TPU v7x, 768 devices: a whole 4x8x12 slice. The times are simulated.
768 devices in a mesh: row: 48 (over y_hi, z, core), col: 16 (over x, y_lo).
Axes of the slice: x: 4, y: 8 (y_hi: 2, y_lo: 4; y = y_hi * 4 + y_lo), z: 12, core: 2. Of those that a mesh axis runs over, the one named last changes fastest.
Arguments:
- tile_left: bfloat16 [48, 16, 2048, 128], P('row', 'col'), may hold values from -6 to 6
- tile_right: bfloat16 [48, 16, 2048, 128], P('row', 'col'), may hold values from -1 to 1
- tile_blocks: int32 [48, 16], P('row', 'col'), may hold values from 1 to 4
- panel_left: bfloat16 [2, 48, 2048, 128], P(None, 'row', 'col'), may hold values from -6 to 6
- panel_right: bfloat16 [2, 48, 2048, 128], P(None, 'row', 'col'), may hold values from -2 to 2
- swap_flag: int32 [48, 16], P('row', 'col'), may hold values from 0 to 1, as said below
Outputs:
- grown_left: bfloat16 [48, 16, 2048, 256], P('row', 'col')
- grown_right: bfloat16 [48, 16, 2048, 256], P('row', 'col')
Inputs may be any that keep to these rules, and one draw needn't show every extreme that they name: swap_flag[i, c] equals swap_flag[i, (c + 16 / 2) mod 16], so tiles change owner in pairs.
All inputs are finite; a program needn't handle non-finite values.
Results may differ from a plain program's by a relative error of at most 0.0057.
Values may be sent and summed in bfloat16 or wider, within the bound.
No kernel may reach another device: no remote copies, remote signals or barrier semaphores. Data moves between devices by JAX's collectives and lax.ppermute only.
A program may use at most 32 MiB of HBM per device.

v0:
```python
import jax
import jax.numpy as jnp
from jax import lax
from jax.sharding import PartitionSpec as P

RBLK = 32


def in_order(parts, dim):
    parts = jnp.moveaxis(parts, 0, dim)
    lengths = parts.shape
    return parts.reshape(*lengths[:dim], lengths[dim] * lengths[dim + 1], *lengths[dim + 2 :])


def copy_for_each(shard, axis):
    size = lax.axis_size(axis)
    return lax.all_to_all(
        jnp.broadcast_to(shard[None], (size, *shard.shape)), axis, 0, 0, tiled=True
    )


def collect_2(shard, axis, dim):
    return in_order(copy_for_each(shard, axis), dim)


def sent_together(arrays, axis, dim, along):
    ends, at = ([], 0)
    for a in arrays[:-1]:
        at += a.shape[along]
        ends.append(at)
    both = jnp.concatenate(arrays, axis=along)
    return tuple(jnp.split(collect_2(both, axis, dim), ends, axis=along))


def sent_together_2(arrays, axis, dim, along):
    widths = [a.shape[along] for a in arrays]
    both = jnp.concatenate(arrays, axis=along)
    filled = lax.all_gather(both, axis, axis=dim, tiled=True)
    return tuple(jnp.split(filled, [sum(widths[:k]) for k in range(1, len(widths))], axis=along))


def sent_together_3(arrays, axis, split_dim, concat_dim, along):
    ends, at = ([], 0)
    for a in arrays[:-1]:
        at += a.shape[along]
        ends.append(at)
    both = jnp.concatenate(arrays, axis=along)
    return tuple(
        jnp.split(
            lax.all_to_all(both, axis, split_axis=split_dim, concat_axis=concat_dim, tiled=True),
            ends,
            axis=along,
        )
    )


def swapped(value, axis, apart):
    mask = 2**apart
    pairs = [(source, source ^ mask) for source in range(lax.axis_size(axis))]
    return lax.ppermute(value, axis, pairs)


def expand(row_left, masked_left, masked_right, col_left, coupling, live_cols):
    lifted = (-jnp.dot(row_left, coupling, preferred_element_type=jnp.float32)).astype(jnp.bfloat16)
    stacked_left = jnp.concatenate([masked_left, lifted], axis=1)
    stacked_right = jnp.concatenate([masked_right, col_left], axis=1)
    dead_cols = jnp.concatenate(
        [1.0 - live_cols.astype(jnp.float32), jnp.zeros((coupling.shape[1],), jnp.float32)]
    )
    gram_matrix = (
        jnp.dot(stacked_left.T, stacked_left, preferred_element_type=jnp.float32)
        / stacked_left.shape[0]
    )
    gram_matrix = gram_matrix + jnp.diag(dead_cols)
    factor = jnp.linalg.cholesky(gram_matrix)
    left_out = lax.linalg.triangular_solve(
        factor, stacked_left.astype(jnp.float32), left_side=False, lower=True, transpose_a=True
    )
    right_out = jnp.dot(stacked_right.astype(jnp.float32), factor, precision=lax.Precision.HIGHEST)
    return (left_out.astype(jnp.bfloat16), right_out.astype(jnp.bfloat16))


def per_device(tile_left, tile_right, tile_blocks, panel_left, panel_right, swap_flag):
    col_count = lax.axis_size("col")
    own_left, own_right = sent_together((panel_left[1], panel_right[1]), "col", 1, 0)
    row_left = own_left[0]
    row_right = own_right[0]
    pieces = sent_together_2((panel_left[0], panel_right[0]), "row", 0, 1)
    count = pieces[0].shape[0]
    source = lax.iota(jnp.int32, count)
    select = (source[:, None] == lax.iota(jnp.int32, col_count)[None, :]).astype(jnp.bfloat16)
    picked_left = jnp.einsum("kc,kbr->cbr", select, pieces[0], preferred_element_type=jnp.float32)
    picked_right = jnp.einsum("kc,kbr->cbr", select, pieces[1], preferred_element_type=jnp.float32)
    held_left = picked_left.astype(jnp.bfloat16)
    held_right = picked_right.astype(jnp.bfloat16)
    whole_left, whole_right = sent_together_3((held_left, held_right), "col", 0, 1, 2)
    col_left = whole_left[0]
    col_right = whole_right[0]
    rank_width = tile_left.shape[3]
    live_mask = lax.iota(jnp.int32, rank_width) < tile_blocks[0, 0] * RBLK
    zero_value = jnp.zeros((), jnp.bfloat16)
    masked_left = jnp.where(live_mask[None, :], tile_left[0, 0], zero_value)
    masked_right = jnp.where(live_mask[None, :], tile_right[0, 0], zero_value)
    coupling = jnp.dot(row_right.T, col_right, preferred_element_type=jnp.float32).astype(
        jnp.bfloat16
    )
    live_cols = live_mask.astype(jnp.bfloat16)
    partner_bit = col_count.bit_length() - 2
    flagged = swap_flag[0, 0] == 1
    arrived = swapped(
        (masked_left, masked_right, col_left, coupling, live_cols), "col", partner_bit
    )
    local_parts = (masked_left, masked_right, col_left, coupling, live_cols)
    chosen_parts = [
        jnp.where(flagged, remote, nearby) for remote, nearby in zip(arrived, local_parts)
    ]
    left_out, right_out = expand(
        row_left,
        chosen_parts[0],
        chosen_parts[1],
        chosen_parts[2],
        chosen_parts[3],
        chosen_parts[4],
    )
    return (left_out[None, None], right_out[None, None])


def solution(mesh):
    placed = (
        P("row", "col", None, None),
        P("row", "col", None, None),
        P("row", "col"),
        P(None, "row", "col", None),
        P(None, "row", "col", None),
        P("row", "col"),
    )
    return jax.shard_map(
        per_device,
        mesh=mesh,
        in_specs=placed,
        out_specs=(P("row", "col", None, None), P("row", "col", None, None)),
        check_vma=False,
    )
```

profile of v0, /device:TPU:1, one launch (start us, length us, event | category | flops | bytes accessed | tf_op | source)
XLA Modules:
  0.0 281.7 jit_solution(1713791106962185055)
XLA Ops:
  7.2 0.8 slice_bitcast_fusion.6
  8.0 0.6 pad_maximum_fusion.3
  8.7 1.2 broadcast_in_dim.55
  9.9 8.0 %all-to-all-start = ((bf16[16,2,128,128]{3,2,1,0:T(8,128)(2,1)}), bf16[16,2,128,128]{3,2,1,0:T(8,128)(2,1)S(1)}, u32[]{:S(2)}, u32[]{:S(2)}) async-start(bf16[16,2,128,128]{3,2,1,0:T(8,128)(2,1)} %broadcast_in_dim.55), calls=%async_computation | async-start | bytes 2097152 | tf_op jit(solution)/shard_map/all_to_all | solution.py:17
  17.9 134.6 %all-gather.2.cloned.1.call-done = bf16[48,256,128]{2,1,0:T(8,128)(2,1)} async-done(((bf16[1,256,128]{2,1,0:T(8,128)(2,1)}), bf16[48,256,128]{2,1,0:T(8,128)(2,1)}) %all-gather.2.cloned.1.call-update) | async-done | bytes 3145744 | tf_op jit(solution)/shard_map/all_gather | solution.py:38
  152.5 2.3 fusion.44
  154.8 1.0 fusion.10
  155.8 1.0 fusion.7
  156.8 0.1 pad_maximum_fusion
  156.9 1.3 copy.23
  158.2 6.1 %all-to-all-start.1 = ((bf16[16,128,256]{2,1,0:T(8,128)(2,1)}), bf16[16,128,256]{2,1,0:T(8,128)(2,1)S(1)}, u32[]{:S(2)}, u32[]{:S(2)}) async-start(bf16[16,128,256]{2,1,0:T(8,128)(2,1)} %copy.23), calls=%async_computation.1 | async-start | bytes 2097152 | tf_op jit(solution)/shard_map/all_to_all | solution.py:50
  165.0 1.0 copy.20
  166.0 1.0 copy.26
  167.0 1.3 bitcast_select_fusion
  168.4 4.8 %collective-permute-start = (bf16[2048,128]{0,1:T(8,128)(2,1)S(1)}, bf16[2048,128]{0,1:T(8,128)(2,1)}, u32[]{:S(2)}, u32[]{:S(2)}) collective-permute-start(bf16[2048,128]{0,1:T(8,128)(2,1)S(1)} %get-tuple-element.39), channel_id=1, source_target_pairs={{0,8},{1,9},{2,10},{3,11},{4,12},{5,13},{6,14},{7,15},{8,0},{9,1},... | collective-permute-start | bytes 1572872 | tf_op jit(solution)/shard_map/ppermute | solution.py:60
  173.2 2.0 collective-permute-start.2
  175.2 4.8 %collective-permute-start.3 = (bf16[2048,128]{0,1:T(8,128)(2,1)S(1)}, bf16[2048,128]{0,1:T(8,128)(2,1)}, u32[]{:S(2)}, u32[]{:S(2)}) collective-permute-start(bf16[2048,128]{0,1:T(8,128)(2,1)S(1)} %get-tuple-element.38), channel_id=1, source_target_pairs={{0,8},{1,9},{2,10},{3,11},{4,12},{5,13},{6,14},{7,15},{8,0},{9,1},... | collective-permute-start | bytes 1572872 | tf_op jit(solution)/shard_map/ppermute | solution.py:60
  180.6 8.7 %collective-permute-done.2 = bf16[128]{0:T(256)(128)(2,1)S(1)} collective-permute-done((bf16[128]{0:T(256)(128)(2,1)S(1)}, bf16[128]{0:T(256)(128)(2,1)S(1)}, u32[]{:S(2)}, u32[]{:S(2)}) %collective-permute-start.2) | collective-permute-done | bytes 288 | tf_op jit(solution)/shard_map/ppermute | solution.py:60
  189.4 1.1 broadcast_select_fusion.2
  190.5 1.1 fusion.45
  191.6 1.4 convolution_convert_fusion.2
  193.0 3.5 %collective-permute-start.1 = (bf16[128,128]{1,0:T(8,128)(2,1)S(1)}, bf16[128,128]{1,0:T(8,128)(2,1)S(1)}, u32[]{:S(2)}, u32[]{:S(2)}) collective-permute-start(bf16[128,128]{1,0:T(8,128)(2,1)S(1)} %convolution_convert_fusion.2), channel_id=1, source_target_pairs={{0,8},{1,9},{2,10},{3,11},{4,12},{5,13},{6,14},{7,15},{8,0},{9,1},... | collective-permute-start | bytes 98312 | tf_op jit(solution)/shard_map/ppermute | solution.py:60
  196.5 5.6 %collective-permute-done.3 = bf16[2048,128]{0,1:T(8,128)(2,1)} collective-permute-done((bf16[2048,128]{0,1:T(8,128)(2,1)S(1)}, bf16[2048,128]{0,1:T(8,128)(2,1)}, u32[]{:S(2)}, u32[]{:S(2)}) %collective-permute-start.3) | collective-permute-done | bytes 524320 | tf_op jit(solution)/shard_map/ppermute | solution.py:60
  202.1 0.2 copy.32
  202.3 3.6 %collective-permute-start.4 = (bf16[2048,128]{0,1:T(8,128)(2,1)S(1)}, bf16[2048,128]{0,1:T(8,128)(2,1)}, u32[]{:S(2)}, u32[]{:S(2)}) collective-permute-start(bf16[2048,128]{0,1:T(8,128)(2,1)S(1)} %bitcast.66), channel_id=1, source_target_pairs={{0,8},{1,9},{2,10},{3,11},{4,12},{5,13},{6,14},{7,15},{8,0},{9,1},... | collective-permute-start | bytes 1572872 | tf_op jit(solution)/shard_map/ppermute | solution.py:60
  206.0 1.4 fusion.1
  207.4 0.5 convolution_multiply_fusion
  207.9 0.1 copy.24
  208.0 0.1 add_multiply_fusion
  208.2 11.7 %cholesky.49 = f32[128,128]{1,0:T(8,128)S(1)} custom-call(f32[128,128]{1,0:T(8,128)S(1)} %cholesky.115), custom_call_target="Cholesky" | custom-call | tf_op jit(solution)/shard_map/jit(cholesky)/cholesky | solution.py:75
  220.0 9.8 %custom-call.14 = f32[1,128,128]{1,2,0:T(8,128)S(1)} custom-call(f32[1,128,128]{2,1,0:T(8,128)S(1)} %get-tuple-element.33), custom_call_target="InvertDiagBlocksLowerTriangular" | custom-call | tf_op jit(solution)/shard_map/jit(cholesky)/cholesky | solution.py:75
  229.8 0.2 constant_dynamic-update-slice_fusion.1
  230.0 0.3 convolution_subtract_fusion
  230.3 11.7 %cholesky.103 = f32[128,128]{1,0:T(8,128)S(1)} custom-call(f32[128,128]{1,0:T(8,128)S(1)} %convolution_subtract_fusion), custom_call_target="Cholesky" | custom-call | tf_op jit(solution)/shard_map/jit(cholesky)/cholesky | solution.py:75
  242.0 0.6 compare_reduce_fusion
  242.6 0.6 compare_reduce_fusion.1
  244.6 4.0 %while.1 = (s32[]{:T(128)}, f32[256,256]{1,0:T(8,128)S(1)}, s32[2,2]{1,0:T(2,128)S(1)}, f32[2,128,128]{2,1,0:T(8,128)S(1)}, s32[]{:T(128)}) while((s32[]{:T(128)}, f32[256,256]{1,0:T(8,128)S(1)}, s32[2,2]{1,0:T(2,128)S(1)}, f32[2,128,128]{2,1,0:T(8,128)S(1)}, s32[]{:T(128)}) %tuple.36), condition=%wide.while_cond, body=%wide.while_body.sunk | while | flops 2 | bytes 131181 | solution.py:76
  244.8 0.6 fusion.53
  245.3 1.3 bitcast_dynamic-update-slice_fusion.2
  246.7 0.6 fusion.53
  247.2 1.3 bitcast_dynamic-update-slice_fusion.2
  248.5 19.7 %custom-call.15 = f32[2,128,128]{1,2,0:T(8,128)S(1)} custom-call(f32[2,128,128]{2,1,0:T(8,128)S(1)} %get-tuple-element.9), custom_call_target="InvertDiagBlocksLowerTriangular" | custom-call | tf_op jit(solution)/shard_map/triangular_solve | solution.py:76
  268.2 0.6 fusion.27
  268.9 1.1 fusion.25
  270.0 1.1 fusion.2
  271.2 0.1 pad_maximum_fusion.1
  271.3 1.3 copy.28
  272.6 2.2 fusion
  (36 shorter events, 0.6 us)
Async XLA Ops:
  7.2 145.4 %all-gather.2.cloned.1.call-start = ((), (), s32[]{:S(2)}) async-start(), calls=%async_computation.2 | async-start | bytes 3211264 | tf_op jit(solution)/shard_map/all_gather | solution.py:38
  9.9 148.3 %all-to-all-start = ((bf16[16,2,128,128]{3,2,1,0:T(8,128)(2,1)}), bf16[16,2,128,128]{3,2,1,0:T(8,128)(2,1)S(1)}, u32[]{:S(2)}, u32[]{:S(2)}) async-start(bf16[16,2,128,128]{3,2,1,0:T(8,128)(2,1)} %broadcast_in_dim.55), calls=%async_computation | async-start | bytes 2097152 | tf_op jit(solution)/shard_map/all_to_all | solution.py:17
  156.9 8.1 %copy-start.3 = (bf16[1,1,2048,128]{3,2,1,0:T(8,128)(2,1)S(1)}, bf16[1,1,2048,128]{3,2,1,0:T(8,128)(2,1)}, u32[]{:S(2)}) copy-start(bf16[1,1,2048,128]{3,2,1,0:T(8,128)(2,1)} %param.6) | copy-start | bytes 1572868
  158.2 7.8 %copy-start.4 = (bf16[1,1,2048,128]{3,2,1,0:T(8,128)(2,1)S(1)}, bf16[1,1,2048,128]{3,2,1,0:T(8,128)(2,1)}, u32[]{:S(2)}) copy-start(bf16[1,1,2048,128]{3,2,1,0:T(8,128)(2,1)} %param.7) | copy-start | bytes 1572868
  158.2 33.4 %all-to-all-start.1 = ((bf16[16,128,256]{2,1,0:T(8,128)(2,1)}), bf16[16,128,256]{2,1,0:T(8,128)(2,1)S(1)}, u32[]{:S(2)}, u32[]{:S(2)}) async-start(bf16[16,128,256]{2,1,0:T(8,128)(2,1)} %copy.23), calls=%async_computation.1 | async-start | bytes 2097152 | tf_op jit(solution)/shard_map/all_to_all | solution.py:50
  168.4 21.0 %copy-start = (bf16[2048,128]{0,1:T(8,128)(2,1)}, bf16[2048,128]{0,1:T(8,128)(2,1)S(1)}, u32[]{:S(2)}) copy-start(bf16[2048,128]{0,1:T(8,128)(2,1)S(1)} %get-tuple-element.39) | copy-start | bytes 1572868
  168.4 21.0 %collective-permute-start = (bf16[2048,128]{0,1:T(8,128)(2,1)S(1)}, bf16[2048,128]{0,1:T(8,128)(2,1)}, u32[]{:S(2)}, u32[]{:S(2)}) collective-permute-start(bf16[2048,128]{0,1:T(8,128)(2,1)S(1)} %get-tuple-element.39), channel_id=1, source_target_pairs={{0,8},{1,9},{2,10},{3,11},{4,12},{5,13},{6,14},{7,15},{8,0},{9,1},... | collective-permute-start | bytes 1572872 | tf_op jit(solution)/shard_map/ppermute | solution.py:60
  173.2 16.2 %collective-permute-start.2 = (bf16[128]{0:T(256)(128)(2,1)S(1)}, bf16[128]{0:T(256)(128)(2,1)S(1)}, u32[]{:S(2)}, u32[]{:S(2)}) collective-permute-start(bf16[128]{0:T(256)(128)(2,1)S(1)} %fusion.42), channel_id=1, source_target_pairs={{0,8},{1,9},{2,10},{3,11},{4,12},{5,13},{6,14},{7,15},{8,0},{9,1},... | collective-permute-start | bytes 776 | tf_op jit(solution)/shard_map/ppermute | solution.py:60
  175.2 26.8 %collective-permute-start.3 = (bf16[2048,128]{0,1:T(8,128)(2,1)S(1)}, bf16[2048,128]{0,1:T(8,128)(2,1)}, u32[]{:S(2)}, u32[]{:S(2)}) collective-permute-start(bf16[2048,128]{0,1:T(8,128)(2,1)S(1)} %get-tuple-element.38), channel_id=1, source_target_pairs={{0,8},{1,9},{2,10},{3,11},{4,12},{5,13},{6,14},{7,15},{8,0},{9,1},... | collective-permute-start | bytes 1572872 | tf_op jit(solution)/shard_map/ppermute | solution.py:60
  193.0 13.0 %collective-permute-start.1 = (bf16[128,128]{1,0:T(8,128)(2,1)S(1)}, bf16[128,128]{1,0:T(8,128)(2,1)S(1)}, u32[]{:S(2)}, u32[]{:S(2)}) collective-permute-start(bf16[128,128]{1,0:T(8,128)(2,1)S(1)} %convolution_convert_fusion.2), channel_id=1, source_target_pairs={{0,8},{1,9},{2,10},{3,11},{4,12},{5,13},{6,14},{7,15},{8,0},{9,1},... | collective-permute-start | bytes 98312 | tf_op jit(solution)/shard_map/ppermute | solution.py:60
  202.3 70.2 %collective-permute-start.4 = (bf16[2048,128]{0,1:T(8,128)(2,1)S(1)}, bf16[2048,128]{0,1:T(8,128)(2,1)}, u32[]{:S(2)}, u32[]{:S(2)}) collective-permute-start(bf16[2048,128]{0,1:T(8,128)(2,1)S(1)} %bitcast.66), channel_id=1, source_target_pairs={{0,8},{1,9},{2,10},{3,11},{4,12},{5,13},{6,14},{7,15},{8,0},{9,1},... | collective-permute-start | bytes 1572872 | tf_op jit(solution)/shard_map/ppermute | solution.py:60
  207.4 0.8 copy-start.1
  268.8 1.2 copy-start.2
Sparse Core Ops, SparseCore 0:
  12.2 140.2 all-gather.1
where the time goes:
time: 287 us; the launch traced here: 282 us
  waiting for transfers between devices  149 us (52%)
  other arithmetic  57.9 us (20%)
  starting transfers between devices  32.8 us (11%)
  between operations  16.9 us (6%)
  local copies, waits for them, and re-layouts  14.3 us (5%)
  matrix products  10.7 us (4%)
    all_gather x1, waiting for transfers between devices, sent_together_2(): filled = lax.all_gather(both, axis, axis=dim, tiled=True)  135 us
    another operation x7, other arithmetic, expand(): factor = jnp.linalg.cholesky(gram_matrix)  34.5 us
    another operation x5, other arithmetic, expand(): lax.linalg.triangular_solve(factor, stacked_left.astype(jnp.float32), lef...  19.9 us
    ppermute x5, starting transfers between devices, swapped(): return lax.ppermute(value, axis, pairs)  18.7 us
    ppermute x5, waiting for transfers between devices, swapped(): return lax.ppermute(value, axis, pairs)  14.3 us
    all_to_all x1, starting transfers between devices, copy_for_each(): lax.all_to_all(jnp.broadcast_to(shard[None], (size, *shard.shape)), axis,...  7.99 us
    all_to_all x1, starting transfers between devices, sent_together_3(): lax.all_to_all(both, axis, split_axis=split_dim, concat_axis=concat_dim,...  6.11 us
  transfers between devices with their start and end apart: 8, of which 3 were waited for; matrix products, arithmetic and copies ran while one was open for 28% of the time, Pallas kernels for 0%

commit v1 on v0

v1 whole, which is shorter than its diff:
```python
import jax
import jax.numpy as jnp
from jax import lax
from jax.experimental import pallas as pl
from jax.experimental.pallas import tpu as pltpu
from jax.sharding import PartitionSpec as P

RBLK = 32
NB = 2048
W = 128
NCOL = 16
NROW = 48
HALF = 64
META = 8
NT = (((1,), (1,)), ((), ()))
NN = (((1,), (0,)), ((), ()))
TN = (((0,), (0,)), ((), ()))
F32 = jnp.float32
BF16 = jnp.bfloat16
HIGH = lax.Precision.HIGHEST


def row_at(y_hi, z, core):
    return y_hi * 24 + z * 2 + core


APART = [[row_at(y, p + 4 * g, k) for y in range(2) for g in range(3) for k in range(2)] for p in range(4)]
RUNS = [[row_at(y, 4 * g + p, k) for p in range(4)] for y in range(2) for g in range(3) for k in range(2)]
CORES = [(r, r ^ 1) for r in range(NROW)]
PARTNERS = [(c, c ^ (NCOL // 2)) for c in range(NCOL)]


def sub(x, m):
    return jnp.broadcast_to(x[m : m + 1, :], x.shape)


def lane(x, m):
    return jnp.broadcast_to(x[:, m : m + 1], (8, W))


def cholesky_and_inverse(a):
    n = a.shape[0] // 8
    ri = lax.broadcasted_iota(jnp.int32, (8, W), 0)
    li = lax.broadcasted_iota(jnp.int32, (8, W), 1)
    rows = [a[8 * g : 8 * g + 8, :] for g in range(n)]
    inv_rows = [jnp.where(li == ri + 8 * g, 1.0, 0.0).astype(F32) for g in range(n)]
    upper, inverse = [], []
    for g in range(n):
        k = 8 * g
        ra, rb = rows[g], inv_rows[g]
        diag = [lane(ra, k + m) for m in range(8)]
        below = {h: [lane(rows[h], k + m) for m in range(8)] for h in range(g + 1, n)}
        ua, ub = ra, rb
        scale = jnp.zeros((8, W), F32)
        for m in range(8):
            r = lax.rsqrt(sub(diag[m], m))
            ba, bb = sub(ra, m), sub(rb, m)
            if m:
                ua = jnp.where(ri == m, ba, ua)
                ub = jnp.where(ri == m, bb, ub)
            scale = jnp.where(ri == m, r, scale)
            c = jnp.where(ri == m, 0.0, diag[m] * (r * r))
            for q in range(m + 1, 8):
                diag[q] = diag[q] - c * sub(diag[q], m)
            ra = ra - c * ba
            rb = rb - c * bb
        upper.append(jnp.where(li >= ri + k, ua * scale, 0.0))
        inverse.append(ub * scale)
        if g + 1 < n:
            qa, qb = ra * (scale * scale), rb * (scale * scale)
            sa = [sub(qa, m) for m in range(8)]
            sb = [sub(qb, m) for m in range(8)]
            for h in range(g + 1, n):
                for m in range(8):
                    rows[h] = rows[h] - below[h][m] * sa[m]
                    inv_rows[h] = inv_rows[h] - below[h][m] * sb[m]
    return jnp.concatenate(upper, 0), jnp.concatenate(inverse, 0)


def dot(a, b, dims, precision=None):
    return lax.dot_general(a, b, dims, precision=precision, preferred_element_type=F32)


FLAG, CORE, PLACE_X, PLACE_Y = range(4)
META = 8
OWN = 2 * W + META


def live_count(at, near, far):
    here, there = near[0, 2 * W : OWN, :].astype(F32), far[0, 2 * W : OWN, :].astype(F32)
    return RBLK * jnp.where(at[0, FLAG] == 1, there, here)[:1, :].astype(jnp.int32)


def first_block(at, own0, own2, near, far, masked, factor_t, factor_inv):
    count = live_count(at, own0, own2)
    live = lax.broadcasted_iota(jnp.int32, (NB, W), 1) < count
    u = jnp.where(at[0, FLAG] == 1, far[...].astype(F32), near[...].astype(F32))
    u = jnp.where(live, u, 0.0).astype(BF16)
    masked[...] = u
    gram = dot(u, u, TN) / NB
    ri = lax.broadcasted_iota(jnp.int32, (W, W), 0)
    li = lax.broadcasted_iota(jnp.int32, (W, W), 1)
    gram = gram + jnp.where((ri == li) & (li >= count), 1.0, 0.0)
    upper, inverse = cholesky_and_inverse(gram)
    factor_t[...] = upper
    factor_inv[...] = inverse


def own_rows(at, pieces, first, whole):
    for t in range(4):
        for s in range(4):
            block = ((at[0, PLACE_X] + t) % 4) * 4 + (at[0, PLACE_Y] + s) % 4
            whole[pl.ds(pl.multiple_of(block * W, W), W), :] = pieces[t][s, first : first + W, :]


def column_rows(at, first_half, second_half, whole):
    for core, ref in ((at[0, CORE], first_half), (1 - at[0, CORE], second_half)):
        for p in range(4):
            for q in range(4):
                block = 8 * (q // 2) + 2 * p + q % 2
                start = pl.multiple_of(block * W + core * HALF, HALF)
                whole[pl.ds(start, HALF), :] = ref(p, q)


def couple(at, own0, own1, own2, own3, near, far, coupling, row_right, col_right):
    own_rows(at, (own0, own1, own2, own3), W, row_right)
    column_rows(at, lambda p, q: near[p, q, HALF:], lambda p, q: far[p, q, HALF:], col_right)
    coupling[...] = dot(row_right[...], col_right[...], TN).astype(BF16)


def parts(x):
    high = x.astype(BF16)
    return high, (x - high.astype(F32)).astype(BF16)


def second_block(
    at, own0, own1, own2, own3, near, far, masked, factor_t, factor_inv, left_out, factor, row_left
):
    own_rows(at, (own0, own1, own2, own3), 0, row_left)
    coupling = jnp.where(at[0, FLAG] == 1, far[...].astype(F32), near[...].astype(F32)).astype(BF16)
    up = (-dot(row_left[...], coupling, NN)).astype(BF16)
    u = masked[...]
    inv11 = factor_inv[...]
    f11t = factor_t[...]
    g12 = dot(u, up, TN) / NB
    g22 = dot(up, up, TN) / NB
    f21t = dot(inv11, g12, NN, HIGH)
    f22t, inv22 = cholesky_and_inverse(g22 - dot(f21t, f21t, TN, HIGH))
    inv21 = -dot(inv22, dot(f21t, inv11, TN, HIGH), NN, HIGH)
    zero = jnp.zeros((W, W), F32)
    factor[...] = jnp.concatenate(
        [jnp.concatenate([f11t, f21t], 1), jnp.concatenate([zero, f22t], 1)], 0
    )
    inverse = jnp.concatenate(
        [jnp.concatenate([inv11, zero], 1), jnp.concatenate([inv21, inv22], 1)], 0
    )
    high, low = parts(inverse)
    row_left[...] = up
    for first in range(0, NB, 512):
        here = pl.ds(first, 512)
        s = jnp.concatenate([masked[here, :], row_left[here, :]], 1)
        left_out[here, :] = (dot(s, high, NT) + dot(s, low, NT)).astype(BF16)


def third_block(
    at, own0, own2, near_right, far_right, near, far, near_swapped, far_swapped, factor, right_out,
    col_left,
):
    flag = at[0, FLAG]

    def either(swapped, kept):
        def read(p, q):
            a, b = swapped[p, q].astype(F32), kept[p, q, :HALF].astype(F32)
            return jnp.where(flag == 1, a, b).astype(BF16)

        return read

    column_rows(at, either(near_swapped, near), either(far_swapped, far), col_left)
    high, low = parts(factor[...])
    live = lax.broadcasted_iota(jnp.int32, (512, W), 1) < live_count(at, own0, own2)
    for first in range(0, NB, 512):
        here = pl.ds(first, 512)
        v = jnp.where(flag == 1, far_right[here, :].astype(F32), near_right[here, :].astype(F32))
        v = jnp.where(live, v, 0.0).astype(BF16)
        t = jnp.concatenate([v, col_left[here, :]], 1)
        right_out[here, :] = (dot(t, high, NT) + dot(t, low, NT)).astype(BF16)


VMEM = pl.BlockSpec(memory_space=pltpu.VMEM)
SMEM = pl.BlockSpec(memory_space=pltpu.SMEM)


def kernel(body, outs, scratch, megaflops, *args):
    return pl.pallas_call(
        body,
        out_shape=[jax.ShapeDtypeStruct(shape, dtype) for shape, dtype in outs],
        in_specs=[SMEM] + [VMEM] * (len(args) - 1),
        out_specs=[VMEM] * len(outs),
        scratch_shapes=[pltpu.VMEM((NB, W), BF16)] * scratch,
        compiler_params=pltpu.CompilerParams(vmem_limit_bytes=32 * 2**20),
        cost_estimate=pl.CostEstimate(
            flops=megaflops * 10**6, bytes_accessed=2**20, transcendentals=0
        ),
    )(*args)


def to_all(x, size, axis, groups):
    return lax.all_to_all(
        jnp.broadcast_to(x[None], (size, *x.shape)).reshape(-1, *x.shape[1:]),
        axis,
        0,
        0,
        tiled=True,
        axis_index_groups=groups,
    )


def per_device(tile_left, tile_right, tile_blocks, panel_left, panel_right, swap_flag):
    row = lax.axis_index("row")
    col = lax.axis_index("col")
    core = row % 2

    blocks = jnp.concatenate(
        [panel_left[0].reshape(2, HALF, W), panel_right[0].reshape(2, HALF, W)], axis=1
    )
    turned = lax.ppermute(
        blocks, ("row", "col"), [(j * NCOL + c, c * NCOL + j) for j in range(NCOL) for c in range(NCOL)]
    )

    counts = jnp.broadcast_to(tile_blocks.astype(BF16), (META, W))
    held = jnp.concatenate([panel_left[1, 0], panel_right[1, 0], counts], 0)
    along_y = [held]
    for s in range(1, 4):
        along_y.append(
            lax.ppermute(held, "col", [(4 * (c // 4) + (c + s) % 4, c) for c in range(NCOL)])
        )
    own = [jnp.stack(along_y)]
    for t in range(1, 4):
        own.append(lax.ppermute(own[0], "col", [((c + 4 * t) % NCOL, c) for c in range(NCOL)]))
    tile_left, tile_right = tile_left[0, 0], tile_right[0, 0]
    tile_left_far = lax.ppermute(tile_left, "col", PARTNERS)
    tile_right_far = lax.ppermute(tile_right, "col", PARTNERS)
    at = jnp.stack([swap_flag[0, 0], core, col // 4, col % 4]).astype(jnp.int32).reshape(1, 4)
    square = ((W, W), F32)
    masked, factor_t, factor_inv = kernel(
        first_block, [((NB, W), BF16), square, square], 0, 6000,
        at, own[0], own[2], tile_left, tile_left_far,
    )

    piece = to_all(turned, 6, "row", APART)[:4]
    piece, own = lax.optimization_barrier((piece, own))
    near = to_all(piece[None], 4, "row", RUNS).reshape(4, 4, W, W)
    near, factor_inv, tile_right_far = lax.optimization_barrier((near, factor_inv, tile_right_far))
    far = lax.ppermute(near, "row", CORES)
    near_swapped = lax.ppermute(near[:, :, :HALF], "col", PARTNERS)
    far_swapped = lax.ppermute(near_swapped, "row", CORES)

    (coupling,) = kernel(couple, [((W, W), BF16)], 2, 2000, at, *own, near, far)
    coupling_far = lax.ppermute(coupling, "col", PARTNERS)
    left_out, factor = kernel(
        second_block, [((NB, 2 * W), BF16), ((2 * W, 2 * W), F32)], 1, 8000,
        at, *own, coupling, coupling_far, masked, factor_t, factor_inv,
    )
    (right_out,) = kernel(
        third_block, [((NB, 2 * W), BF16)], 1, 2000,
        at, own[0], own[2], tile_right, tile_right_far, near, far, near_swapped, far_swapped, factor,
    )
    return left_out[None, None], right_out[None, None]


def solution(mesh):
    placed = (
        P("row", "col", None, None),
        P("row", "col", None, None),
        P("row", "col"),
        P(None, "row", "col", None),
        P(None, "row", "col", None),
        P("row", "col"),
    )
    return jax.shard_map(
        per_device,
        mesh=mesh,
        in_specs=placed,
        out_specs=(P("row", "col", None, None), P("row", "col", None, None)),
        check_vma=False,
    )
```

time: 287 us -> 138 us (0.48); the launches traced: 282 us -> 137 us
  waiting for transfers between devices: 149 us -> 37.1 us
  other arithmetic: 57.9 us -> 0.22 us
  starting transfers between devices: 32.8 us -> 76.4 us
  Pallas kernels: 0 us -> 16.9 us
  between operations: 16.9 us -> 2.23 us
  matrix products: 10.7 us -> 0 us
  local copies, waits for them, and re-layouts: 14.3 us -> 4.01 us
    all_gather x1 -> x0, waiting for transfers between devices: 135 us -> none  [sent_together_2(): filled = lax.all_gather(both, axis, axis=dim, tiled=True)]
    another operation x12 -> x2, other arithmetic: 54.4 us -> 0.14 us  [per_device(): own = [jnp.stack(along_y)]]
    ppermute x5 -> x13, starting transfers between devices: 18.7 us -> 48.6 us  [the longest x3 16.5 us: per_device(): lax.ppermute(held, 'col', [(4 * (c // 4) + (c + s) % 4, c) for c in range...]
    ppermute x5 -> x13, waiting for transfers between devices: 14.3 us -> 37.1 us  [the longest x3 12.9 us: per_device(): lax.ppermute(own[0], 'col', [((c + 4 * t) % NCOL, c) for c in range(NCOL)])]
    pallas_call x0 -> x4, Pallas kernels: none -> 16.9 us  [kernel(): pl.pallas_call(body, out_shape=[jax.ShapeDtypeStruct(shape, dtype) for sh...]
    all_to_all x2, starting transfers between devices: 14.1 us -> 27.8 us  [to_all(): lax.all_to_all(jnp.broadcast_to(x[None], (size, *x.shape)).reshape(-1, *x...]
    dot_general x6 -> x0, matrix products: 7.37 us -> none  [the longest x1 2.19 us: expand(): jnp.dot(stacked_right.astype(jnp.float32), factor, precision=lax.Precisio...]
    another operation x9 -> x0, local copies, waits for them, and re-layouts: 3.85 us -> none
  transfers between devices with their start and end apart: 8 -> 15, of which waited for: 3 -> 8; matrix products, arithmetic and copies ran while one was open for 28% -> 0% of each run, Pallas kernels for 0% -> 11%
where the time goes in v1:
time: 138 us; the launch traced here: 137 us
  starting transfers between devices  76.4 us (55%)
  waiting for transfers between devices  37.1 us (27%)
  Pallas kernels  16.9 us (12%)
  local copies, waits for them, and re-layouts  4.01 us (3%)
  between operations  2.23 us (2%)
    all_to_all x2, starting transfers between devices, to_all(): lax.all_to_all(jnp.broadcast_to(x[None], (size, *x.shape)).reshape(-1, *x...  27.8 us
    pallas_call x4, Pallas kernels, kernel(): pl.pallas_call(body, out_shape=[jax.ShapeDtypeStruct(shape, dtype) for sh...  16.9 us
    ppermute x3, starting transfers between devices, per_device(): lax.ppermute(held, 'col', [(4 * (c // 4) + (c + s) % 4, c) for c in range...  16.5 us
    ppermute x3, waiting for transfers between devices, per_device(): lax.ppermute(own[0], 'col', [((c + 4 * t) % NCOL, c) for c in range(NCOL)])  12.9 us
    ppermute x1, waiting for transfers between devices, per_device(): tile_left_far = lax.ppermute(tile_left, 'col', PARTNERS)  8.51 us
    ppermute x3, starting transfers between devices, per_device(): lax.ppermute(own[0], 'col', [((c + 4 * t) % NCOL, c) for c in range(NCOL)])  7.21 us
    ppermute x3, waiting for transfers between devices, per_device(): lax.ppermute(held, 'col', [(4 * (c // 4) + (c + s) % 4, c) for c in range...  5.78 us
    ppermute x1, starting transfers between devices, per_device(): lax.ppermute(blocks, ('row', 'col'), [(j * NCOL + c, c * NCOL + j) for j...  4.59 us
  transfers between devices with their start and end apart: 15, of which 8 were waited for; matrix products, arithmetic and copies ran while one was open for 0% of the time, Pallas kernels for 11%

profile of v1, /device:TPU:1, one launch (start us, length us, event | category | flops | bytes accessed | tf_op | source)
XLA Modules:
  0.0 136.9 jit_solution(12190301115652495604)
XLA Ops:
  0.6 0.8 slice_bitcast_fusion
  1.5 4.6 %collective-permute-start = (bf16[2,128,128]{2,1,0:T(8,128)(2,1)S(1)}, bf16[2,128,128]{2,1,0:T(8,128)(2,1)S(1)}, u32[]{:S(2)}, u32[]{:S(2)}) collective-permute-start(bf16[2,128,128]{2,1,0:T(8,128)(2,1)S(1)} %pad_maximum_fusion.1), channel_id=1, source_target_pairs={{0,0},{1,16},{2,32},{3,48},{4,64},{5,80},{6,96},{7,112},{8,128},{9... | collective-permute-start | bytes 196616 | tf_op jit(solution)/shard_map/ppermute | solution.py:226
  6.1 1.9 %collective-permute-done = bf16[2,128,128]{2,1,0:T(8,128)(2,1)S(1)} collective-permute-done((bf16[2,128,128]{2,1,0:T(8,128)(2,1)S(1)}, bf16[2,128,128]{2,1,0:T(8,128)(2,1)S(1)}, u32[]{:S(2)}, u32[]{:S(2)}) %collective-permute-start) | collective-permute-done | bytes 65568 | tf_op jit(solution)/shard_map/ppermute | solution.py:226
  8.0 0.8 broadcast_in_dim.10
  8.8 18.4 %all-to-all-start = ((bf16[12,128,128]{2,1,0:T(8,128)(2,1)}), bf16[12,128,128]{2,1,0:T(8,128)(2,1)S(1)}, u32[]{:S(2)}, u32[]{:S(2)}) async-start(bf16[12,128,128]{2,1,0:T(8,128)(2,1)} %bitcast.7), calls=%async_computation | async-start | bytes 786432 | tf_op jit(solution)/shard_map/all_to_all | solution.py:208
  27.9 0.1 fusion
  28.1 5.0 %collective-permute-start.3 = (bf16[264,128]{1,0:T(8,128)(2,1)S(1)}, bf16[264,128]{1,0:T(8,128)(2,1)S(1)}, u32[]{:S(2)}, u32[]{:S(2)}) collective-permute-start(bf16[264,128]{1,0:T(8,128)(2,1)S(1)} %get-tuple-element.29), channel_id=1, source_target_pairs={{3,0},{0,1},{1,2},{2,3},{7,4},{4,5},{5,6},{6,7},{11,8},{8,9},{9,10... | collective-permute-start | bytes 202760 | tf_op jit(solution)/shard_map/ppermute | solution.py:235
  33.1 8.5 %collective-permute-start.2 = (bf16[264,128]{1,0:T(8,128)(2,1)S(1)}, bf16[264,128]{1,0:T(8,128)(2,1)S(1)}, u32[]{:S(2)}, u32[]{:S(2)}) collective-permute-start(bf16[264,128]{1,0:T(8,128)(2,1)S(1)} %get-tuple-element.29), channel_id=1, source_target_pairs={{2,0},{3,1},{0,2},{1,3},{6,4},{7,5},{4,6},{5,7},{10,8},{11,9},{8,1... | collective-permute-start | bytes 202760 | tf_op jit(solution)/shard_map/ppermute | solution.py:235
  41.6 2.9 %collective-permute-start.1 = (bf16[264,128]{1,0:T(8,128)(2,1)S(1)}, bf16[264,128]{1,0:T(8,128)(2,1)S(1)}, u32[]{:S(2)}, u32[]{:S(2)}) collective-permute-start(bf16[264,128]{1,0:T(8,128)(2,1)S(1)} %get-tuple-element.29), channel_id=1, source_target_pairs={{1,0},{2,1},{3,2},{0,3},{5,4},{6,5},{7,6},{4,7},{9,8},{10,9},{11,1... | collective-permute-start | bytes 202760 | tf_op jit(solution)/shard_map/ppermute | solution.py:235
  44.6 0.0 collective-permute-done.3
  44.6 5.8 %collective-permute-done.2 = bf16[264,128]{1,0:T(8,128)(2,1)S(1)} collective-permute-done((bf16[264,128]{1,0:T(8,128)(2,1)S(1)}, bf16[264,128]{1,0:T(8,128)(2,1)S(1)}, u32[]{:S(2)}, u32[]{:S(2)}) %collective-permute-start.2) | collective-permute-done | bytes 67616 | tf_op jit(solution)/shard_map/ppermute | solution.py:235
  50.4 0.0 collective-permute-done.1
  50.4 2.6 %collective-permute-start.4 = (bf16[4,264,128]{2,1,0:T(8,128)(2,1)S(1)}, bf16[4,264,128]{2,1,0:T(8,128)(2,1)S(1)}, u32[]{:S(2)}, u32[]{:S(2)}) collective-permute-start(bf16[4,264,128]{2,1,0:T(8,128)(2,1)S(1)} %pad_maximum_fusion.own0), channel_id=1, source_target_pairs={{4,0},{5,1},{6,2},{7,3},{8,4},{9,5},{10,6},{11,7},{12,8},{13,9},{1... | collective-permute-start | bytes 811016 | tf_op jit(solution)/shard_map/ppermute | solution.py:239
  53.0 2.7 %collective-permute-start.5 = (bf16[4,264,128]{2,1,0:T(8,128)(2,1)S(1)}, bf16[4,264,128]{2,1,0:T(8,128)(2,1)S(1)}, u32[]{:S(2)}, u32[]{:S(2)}) collective-permute-start(bf16[4,264,128]{2,1,0:T(8,128)(2,1)S(1)} %pad_maximum_fusion.own0), channel_id=1, source_target_pairs={{8,0},{9,1},{10,2},{11,3},{12,4},{13,5},{14,6},{15,7},{0,8},{1,9},... | collective-permute-start | bytes 811016 | tf_op jit(solution)/shard_map/ppermute | solution.py:239
  55.7 1.9 %collective-permute-start.6 = (bf16[4,264,128]{2,1,0:T(8,128)(2,1)S(1)}, bf16[4,264,128]{2,1,0:T(8,128)(2,1)S(1)}, u32[]{:S(2)}, u32[]{:S(2)}) collective-permute-start(bf16[4,264,128]{2,1,0:T(8,128)(2,1)S(1)} %pad_maximum_fusion.own0), channel_id=1, source_target_pairs={{12,0},{13,1},{14,2},{15,3},{0,4},{1,5},{2,6},{3,7},{4,8},{5,9},{6... | collective-permute-start | bytes 811016 | tf_op jit(solution)/shard_map/ppermute | solution.py:239
  57.6 0.0 all-to-all-done
  57.7 2.2 %collective-permute-done.4.own1 = bf16[4,264,128]{2,1,0:T(8,128)(2,1)S(1)} collective-permute-done((bf16[4,264,128]{2,1,0:T(8,128)(2,1)S(1)}, bf16[4,264,128]{2,1,0:T(8,128)(2,1)S(1)}, u32[]{:S(2)}, u32[]{:S(2)}) %collective-permute-start.4) | collective-permute-done | bytes 270368 | tf_op jit(solution)/shard_map/ppermute | solution.py:239
  59.9 3.7 %collective-permute-done.5.own2 = bf16[4,264,128]{2,1,0:T(8,128)(2,1)S(1)} collective-permute-done((bf16[4,264,128]{2,1,0:T(8,128)(2,1)S(1)}, bf16[4,264,128]{2,1,0:T(8,128)(2,1)S(1)}, u32[]{:S(2)}, u32[]{:S(2)}) %collective-permute-start.5) | collective-permute-done | bytes 270368 | tf_op jit(solution)/shard_map/ppermute | solution.py:239
  63.6 7.0 %collective-permute-done.6.own3 = bf16[4,264,128]{2,1,0:T(8,128)(2,1)S(1)} collective-permute-done((bf16[4,264,128]{2,1,0:T(8,128)(2,1)S(1)}, bf16[4,264,128]{2,1,0:T(8,128)(2,1)S(1)}, u32[]{:S(2)}, u32[]{:S(2)}) %collective-permute-start.6) | collective-permute-done | bytes 270368 | tf_op jit(solution)/shard_map/ppermute | solution.py:239
  70.6 0.9 reshape.19
  71.5 0.0 copy-done.2
  71.5 9.4 %all-to-all-start.1 = ((bf16[4,4,128,128]{3,2,1,0:T(8,128)(2,1)}), bf16[4,4,128,128]{3,2,1,0:T(8,128)(2,1)S(1)}, u32[]{:S(2)}, u32[]{:S(2)}) async-start(bf16[4,4,128,128]{3,2,1,0:T(8,128)(2,1)} %reshape.19), calls=%async_computation.1 | async-start | bytes 1048576 | tf_op jit(solution)/shard_map/all_to_all | solution.py:208
  80.8 0.0 copy-done
  80.8 3.2 %collective-permute-start.7 = (bf16[2048,128]{1,0:T(8,128)(2,1)S(1)}, bf16[2048,128]{1,0:T(8,128)(2,1)S(1)}, u32[]{:S(2)}, u32[]{:S(2)}) collective-permute-start(bf16[2048,128]{1,0:T(8,128)(2,1)S(1)} %bitcast.24), channel_id=1, source_target_pairs={{0,8},{1,9},{2,10},{3,11},{4,12},{5,13},{6,14},{7,15},{8,0},{9,1},... | collective-permute-start | bytes 1572872 | tf_op jit(solution)/shard_map/ppermute | solution.py:241
  84.0 0.0 copy-done.1
  84.1 3.6 %collective-permute-start.8 = (bf16[2048,128]{1,0:T(8,128)(2,1)S(1)}, bf16[2048,128]{1,0:T(8,128)(2,1)S(1)}, u32[]{:S(2)}, u32[]{:S(2)}) collective-permute-start(bf16[2048,128]{1,0:T(8,128)(2,1)S(1)} %bitcast.26), channel_id=1, source_target_pairs={{0,8},{1,9},{2,10},{3,11},{4,12},{5,13},{6,14},{7,15},{8,0},{9,1},... | collective-permute-start | bytes 1572872 | tf_op jit(solution)/shard_map/ppermute | solution.py:242
  88.3 0.1 add_bitcast_fusion.at
  88.4 8.5 %collective-permute-done.7.far = bf16[2048,128]{1,0:T(8,128)(2,1)S(1)} collective-permute-done((bf16[2048,128]{1,0:T(8,128)(2,1)S(1)}, bf16[2048,128]{1,0:T(8,128)(2,1)S(1)}, u32[]{:S(2)}, u32[]{:S(2)}) %collective-permute-start.7) | collective-permute-done | bytes 524320 | tf_op jit(solution)/shard_map/ppermute | solution.py:241
  96.9 5.4 %shard_map.77 = (bf16[2048,128]{1,0:T(8,128)(2,1)S(1)}, f32[128,128]{1,0:T(8,128)S(1)}, f32[128,128]{1,0:T(8,128)S(1)}) custom-call(s32[1,4]{1,0:T(1,128)S(1)} %add_bitcast_fusion.at, bf16[4,264,128]{2,1,0:T(8,128)(2,1)S(1)} %pad_maximum_fusion.own0, bf16[4,264,128]{2,1,0:T(8,128)(2,1)S(1)} %collective-permute-done.5.own2, bf16[2048,128]{1,0:T(8,128)(2,1)S(1)} %bitcast.25, ...), custom_call_target="tpu_custom_call" | custom-call | flops 6000000000 | bytes 1048576 | tf_op jit(solution)/shard_map/pallas_call | solution.py:194
  102.3 0.0 copy-start.4
  102.3 0.8 copy-done.4
  103.1 0.6 copy-done.6
  103.7 4.4 %collective-permute-done.8.far_right = bf16[2048,128]{1,0:T(8,128)(2,1)S(1)} collective-permute-done((bf16[2048,128]{1,0:T(8,128)(2,1)S(1)}, bf16[2048,128]{1,0:T(8,128)(2,1)S(1)}, u32[]{:S(2)}, u32[]{:S(2)}) %collective-permute-start.8) | collective-permute-done | bytes 524320 | tf_op jit(solution)/shard_map/ppermute | solution.py:242
  108.1 0.0 all-to-all-done.1.near
  108.1 3.6 %collective-permute-start.9 = (bf16[4,4,128,128]{3,2,1,0:T(8,128)(2,1)S(1)}, bf16[4,4,128,128]{3,2,1,0:T(8,128)(2,1)S(1)}, u32[]{:S(2)}, u32[]{:S(2)}) collective-permute-start(bf16[4,4,128,128]{3,2,1,0:T(8,128)(2,1)S(1)} %all-to-all-done.1.near), channel_id=1, source_target_pairs={{0,16},{16,0},{32,48},{48,32},{64,80},{80,64},{96,112},{112,96},{1... | collective-permute-start | bytes 1572872 | tf_op jit(solution)/shard_map/ppermute | solution.py:254
  111.7 0.0 copy-start.5
  111.7 0.0 copy-start.7
  111.8 3.3 %collective-permute-start.11 = (bf16[4,4,64,128]{3,2,1,0:T(8,128)(2,1)S(1)}, bf16[4,4,64,128]{3,2,1,0:T(8,128)(2,1)S(1)}, u32[]{:S(2)}, u32[]{:S(2)}) collective-permute-start(bf16[4,4,64,128]{3,2,1,0:T(8,128)(2,1)S(1)} %slice.23), channel_id=1, source_target_pairs={{0,8},{1,9},{2,10},{3,11},{4,12},{5,13},{6,14},{7,15},{8,0},{9,1},... | collective-permute-start | bytes 786440 | tf_op jit(solution)/shard_map/ppermute | solution.py:255
  115.1 0.0 collective-permute-done.9.far
  115.1 0.0 copy-done.3
  115.1 0.9 shard_map.78.near
  116.1 3.6 %collective-permute-start.10 = (bf16[128,128]{1,0:T(8,128)(2,1)S(1)}, bf16[128,128]{1,0:T(8,128)(2,1)S(1)}, u32[]{:S(2)}, u32[]{:S(2)}) collective-permute-start(bf16[128,128]{1,0:T(8,128)(2,1)S(1)} %shard_map.78.near), channel_id=1, source_target_pairs={{0,8},{1,9},{2,10},{3,11},{4,12},{5,13},{6,14},{7,15},{8,0},{9,1},... | collective-permute-start | bytes 98312 | tf_op jit(solution)/shard_map/ppermute | solution.py:259
  119.7 3.5 %collective-permute-done.11.near_swapped = bf16[4,4,64,128]{3,2,1,0:T(8,128)(2,1)S(1)} collective-permute-done((bf16[4,4,64,128]{3,2,1,0:T(8,128)(2,1)S(1)}, bf16[4,4,64,128]{3,2,1,0:T(8,128)(2,1)S(1)}, u32[]{:S(2)}, u32[]{:S(2)}) %collective-permute-start.11) | collective-permute-done | bytes 262176 | tf_op jit(solution)/shard_map/ppermute | solution.py:255
  123.2 3.0 %collective-permute-start.12 = (bf16[4,4,64,128]{3,2,1,0:T(8,128)(2,1)S(1)}, bf16[4,4,64,128]{3,2,1,0:T(8,128)(2,1)S(1)}, u32[]{:S(2)}, u32[]{:S(2)}) collective-permute-start(bf16[4,4,64,128]{3,2,1,0:T(8,128)(2,1)S(1)} %collective-permute-done.11.near_swapped), channel_id=1, source_target_pairs={{0,16},{16,0},{32,48},{48,32},{64,80},{80,64},{96,112},{112,96},{1... | collective-permute-start | bytes 786440 | tf_op jit(solution)/shard_map/ppermute | solution.py:256
  126.3 0.0 collective-permute-done.10.far
  126.3 8.2 %shard_map.79 = (bf16[2048,256]{1,0:T(8,128)(2,1)}, f32[256,256]{1,0:T(8,128)S(1)}) custom-call(s32[1,4]{1,0:T(1,128)S(1)} %add_bitcast_fusion.at, bf16[4,264,128]{2,1,0:T(8,128)(2,1)S(1)} %pad_maximum_fusion.own0, bf16[4,264,128]{2,1,0:T(8,128)(2,1)S(1)} %collective-permute-done.4.own1, bf16[4,264,128]{2,1,0:T(8,128)(2,1)S(1)} %collective-permute-done.5.own2, ...), custom_call_target="tpu_custom_call" | custom-call | flops 8000000000 | bytes 1048576 | tf_op jit(solution)/shard_map/pallas_call | solution.py:194
  134.5 0.0 collective-permute-done.12.far_swapped
  134.5 2.4 %shard_map.80 = bf16[2048,256]{1,0:T(8,128)(2,1)} custom-call(s32[1,4]{1,0:T(1,128)S(1)} %add_bitcast_fusion.at, bf16[4,264,128]{2,1,0:T(8,128)(2,1)S(1)} %pad_maximum_fusion.own0, bf16[4,264,128]{2,1,0:T(8,128)(2,1)S(1)} %collective-permute-done.5.own2, bf16[2048,128]{1,0:T(8,128)(2,1)S(1)} %bitcast.27, ...), custom_call_target="tpu_custom_call" | custom-call | flops 2000000000 | bytes 1048576 | tf_op jit(solution)/shard_map/pallas_call | solution.py:194
  (13 shorter events, 0.1 us)
Async XLA Ops:
  1.5 6.5 %collective-permute-start = (bf16[2,128,128]{2,1,0:T(8,128)(2,1)S(1)}, bf16[2,128,128]{2,1,0:T(8,128)(2,1)S(1)}, u32[]{:S(2)}, u32[]{:S(2)}) collective-permute-start(bf16[2,128,128]{2,1,0:T(8,128)(2,1)S(1)} %pad_maximum_fusion.1), channel_id=1, source_target_pairs={{0,0},{1,16},{2,32},{3,48},{4,64},{5,80},{6,96},{7,112},{8,128},{9... | collective-permute-start | bytes 196616 | tf_op jit(solution)/shard_map/ppermute | solution.py:226
  8.8 48.8 %all-to-all-start = ((bf16[12,128,128]{2,1,0:T(8,128)(2,1)}), bf16[12,128,128]{2,1,0:T(8,128)(2,1)S(1)}, u32[]{:S(2)}, u32[]{:S(2)}) async-start(bf16[12,128,128]{2,1,0:T(8,128)(2,1)} %bitcast.7), calls=%async_computation | async-start | bytes 786432 | tf_op jit(solution)/shard_map/all_to_all | solution.py:208
  28.1 16.5 %collective-permute-start.3 = (bf16[264,128]{1,0:T(8,128)(2,1)S(1)}, bf16[264,128]{1,0:T(8,128)(2,1)S(1)}, u32[]{:S(2)}, u32[]{:S(2)}) collective-permute-start(bf16[264,128]{1,0:T(8,128)(2,1)S(1)} %get-tuple-element.29), channel_id=1, source_target_pairs={{3,0},{0,1},{1,2},{2,3},{7,4},{4,5},{5,6},{6,7},{11,8},{8,9},{9,10... | collective-permute-start | bytes 202760 | tf_op jit(solution)/shard_map/ppermute | solution.py:235
  33.1 17.3 %collective-permute-start.2 = (bf16[264,128]{1,0:T(8,128)(2,1)S(1)}, bf16[264,128]{1,0:T(8,128)(2,1)S(1)}, u32[]{:S(2)}, u32[]{:S(2)}) collective-permute-start(bf16[264,128]{1,0:T(8,128)(2,1)S(1)} %get-tuple-element.29), channel_id=1, source_target_pairs={{2,0},{3,1},{0,2},{1,3},{6,4},{7,5},{4,6},{5,7},{10,8},{11,9},{8,1... | collective-permute-start | bytes 202760 | tf_op jit(solution)/shard_map/ppermute | solution.py:235
  41.6 8.7 %collective-permute-start.1 = (bf16[264,128]{1,0:T(8,128)(2,1)S(1)}, bf16[264,128]{1,0:T(8,128)(2,1)S(1)}, u32[]{:S(2)}, u32[]{:S(2)}) collective-permute-start(bf16[264,128]{1,0:T(8,128)(2,1)S(1)} %get-tuple-element.29), channel_id=1, source_target_pairs={{1,0},{2,1},{3,2},{0,3},{5,4},{6,5},{7,6},{4,7},{9,8},{10,9},{11,1... | collective-permute-start | bytes 202760 | tf_op jit(solution)/shard_map/ppermute | solution.py:235
  50.4 9.5 %collective-permute-start.4 = (bf16[4,264,128]{2,1,0:T(8,128)(2,1)S(1)}, bf16[4,264,128]{2,1,0:T(8,128)(2,1)S(1)}, u32[]{:S(2)}, u32[]{:S(2)}) collective-permute-start(bf16[4,264,128]{2,1,0:T(8,128)(2,1)S(1)} %pad_maximum_fusion.own0), channel_id=1, source_target_pairs={{4,0},{5,1},{6,2},{7,3},{8,4},{9,5},{10,6},{11,7},{12,8},{13,9},{1... | collective-permute-start | bytes 811016 | tf_op jit(solution)/shard_map/ppermute | solution.py:239
  53.0 10.6 %collective-permute-start.5 = (bf16[4,264,128]{2,1,0:T(8,128)(2,1)S(1)}, bf16[4,264,128]{2,1,0:T(8,128)(2,1)S(1)}, u32[]{:S(2)}, u32[]{:S(2)}) collective-permute-start(bf16[4,264,128]{2,1,0:T(8,128)(2,1)S(1)} %pad_maximum_fusion.own0), channel_id=1, source_target_pairs={{8,0},{9,1},{10,2},{11,3},{12,4},{13,5},{14,6},{15,7},{0,8},{1,9},... | collective-permute-start | bytes 811016 | tf_op jit(solution)/shard_map/ppermute | solution.py:239
  55.7 14.9 %collective-permute-start.6 = (bf16[4,264,128]{2,1,0:T(8,128)(2,1)S(1)}, bf16[4,264,128]{2,1,0:T(8,128)(2,1)S(1)}, u32[]{:S(2)}, u32[]{:S(2)}) collective-permute-start(bf16[4,264,128]{2,1,0:T(8,128)(2,1)S(1)} %pad_maximum_fusion.own0), channel_id=1, source_target_pairs={{12,0},{13,1},{14,2},{15,3},{0,4},{1,5},{2,6},{3,7},{4,8},{5,9},{6... | collective-permute-start | bytes 811016 | tf_op jit(solution)/shard_map/ppermute | solution.py:239
  70.6 0.9 copy-start.2
  71.5 9.4 %copy-start = (bf16[1,1,2048,128]{3,2,1,0:T(8,128)(2,1)S(1)}, bf16[1,1,2048,128]{3,2,1,0:T(8,128)(2,1)}, u32[]{:S(2)}) copy-start(bf16[1,1,2048,128]{3,2,1,0:T(8,128)(2,1)} %param.6) | copy-start | bytes 1572868
  71.5 12.6 %copy-start.1 = (bf16[1,1,2048,128]{3,2,1,0:T(8,128)(2,1)S(1)}, bf16[1,1,2048,128]{3,2,1,0:T(8,128)(2,1)}, u32[]{:S(2)}) copy-start(bf16[1,1,2048,128]{3,2,1,0:T(8,128)(2,1)} %param.7) | copy-start | bytes 1572868
  71.5 36.7 %all-to-all-start.1 = ((bf16[4,4,128,128]{3,2,1,0:T(8,128)(2,1)}), bf16[4,4,128,128]{3,2,1,0:T(8,128)(2,1)S(1)}, u32[]{:S(2)}, u32[]{:S(2)}) async-start(bf16[4,4,128,128]{3,2,1,0:T(8,128)(2,1)} %reshape.19), calls=%async_computation.1 | async-start | bytes 1048576 | tf_op jit(solution)/shard_map/all_to_all | solution.py:208
  80.8 16.1 %collective-permute-start.7 = (bf16[2048,128]{1,0:T(8,128)(2,1)S(1)}, bf16[2048,128]{1,0:T(8,128)(2,1)S(1)}, u32[]{:S(2)}, u32[]{:S(2)}) collective-permute-start(bf16[2048,128]{1,0:T(8,128)(2,1)S(1)} %bitcast.24), channel_id=1, source_target_pairs={{0,8},{1,9},{2,10},{3,11},{4,12},{5,13},{6,14},{7,15},{8,0},{9,1},... | collective-permute-start | bytes 1572872 | tf_op jit(solution)/shard_map/ppermute | solution.py:241
  84.1 24.1 %collective-permute-start.8 = (bf16[2048,128]{1,0:T(8,128)(2,1)S(1)}, bf16[2048,128]{1,0:T(8,128)(2,1)S(1)}, u32[]{:S(2)}, u32[]{:S(2)}) collective-permute-start(bf16[2048,128]{1,0:T(8,128)(2,1)S(1)} %bitcast.26), channel_id=1, source_target_pairs={{0,8},{1,9},{2,10},{3,11},{4,12},{5,13},{6,14},{7,15},{8,0},{9,1},... | collective-permute-start | bytes 1572872 | tf_op jit(solution)/shard_map/ppermute | solution.py:242
  102.3 0.8 copy-start.4
  103.1 0.6 copy-start.6
  103.7 11.4 %copy-start.3 = (bf16[4,264,128]{2,1,0:T(8,128)(2,1)S(1)}, bf16[4,264,128]{2,1,0:T(8,128)(2,1)}, u32[]{:S(2)}) copy-start(bf16[4,264,128]{2,1,0:T(8,128)(2,1)} %copy-done.2) | copy-start | bytes 811012
  108.1 7.0 %collective-permute-start.9 = (bf16[4,4,128,128]{3,2,1,0:T(8,128)(2,1)S(1)}, bf16[4,4,128,128]{3,2,1,0:T(8,128)(2,1)S(1)}, u32[]{:S(2)}, u32[]{:S(2)}) collective-permute-start(bf16[4,4,128,128]{3,2,1,0:T(8,128)(2,1)S(1)} %all-to-all-done.1.near), channel_id=1, source_target_pairs={{0,16},{16,0},{32,48},{48,32},{64,80},{80,64},{96,112},{112,96},{1... | collective-permute-start | bytes 1572872 | tf_op jit(solution)/shard_map/ppermute | solution.py:254
  111.7 14.5 %copy-start.5 = (bf16[2048,128]{1,0:T(8,128)(2,1)S(1)}, bf16[2048,128]{1,0:T(8,128)(2,1)}, u32[]{:S(2)}) copy-start(bf16[2048,128]{1,0:T(8,128)(2,1)} %copy-done.4) | copy-start | bytes 1572868
  111.7 14.5 %copy-start.7 = (f32[128,128]{1,0:T(8,128)S(1)}, f32[128,128]{1,0:T(8,128)}, u32[]{:S(2)}) copy-start(f32[128,128]{1,0:T(8,128)} %copy-done.6) | copy-start | bytes 196612
  111.8 11.5 %collective-permute-start.11 = (bf16[4,4,64,128]{3,2,1,0:T(8,128)(2,1)S(1)}, bf16[4,4,64,128]{3,2,1,0:T(8,128)(2,1)S(1)}, u32[]{:S(2)}, u32[]{:S(2)}) collective-permute-start(bf16[4,4,64,128]{3,2,1,0:T(8,128)(2,1)S(1)} %slice.23), channel_id=1, source_target_pairs={{0,8},{1,9},{2,10},{3,11},{4,12},{5,13},{6,14},{7,15},{8,0},{9,1},... | collective-permute-start | bytes 786440 | tf_op jit(solution)/shard_map/ppermute | solution.py:255
  116.1 10.2 %collective-permute-start.10 = (bf16[128,128]{1,0:T(8,128)(2,1)S(1)}, bf16[128,128]{1,0:T(8,128)(2,1)S(1)}, u32[]{:S(2)}, u32[]{:S(2)}) collective-permute-start(bf16[128,128]{1,0:T(8,128)(2,1)S(1)} %shard_map.78.near), channel_id=1, source_target_pairs={{0,8},{1,9},{2,10},{3,11},{4,12},{5,13},{6,14},{7,15},{8,0},{9,1},... | collective-permute-start | bytes 98312 | tf_op jit(solution)/shard_map/ppermute | solution.py:259
  123.2 11.3 %collective-permute-start.12 = (bf16[4,4,64,128]{3,2,1,0:T(8,128)(2,1)S(1)}, bf16[4,4,64,128]{3,2,1,0:T(8,128)(2,1)S(1)}, u32[]{:S(2)}, u32[]{:S(2)}) collective-permute-start(bf16[4,4,64,128]{3,2,1,0:T(8,128)(2,1)S(1)} %collective-permute-done.11.near_swapped), channel_id=1, source_target_pairs={{0,16},{16,0},{32,48},{48,32},{64,80},{80,64},{96,112},{112,96},{1... | collective-permute-start | bytes 786440 | tf_op jit(solution)/shard_map/ppermute | solution.py:256

commit v2 on v1

v2 whole, which is shorter than its diff:
```python
import jax
import jax.numpy as jnp
from jax import lax
from jax.experimental import pallas as pl
from jax.experimental.pallas import tpu as pltpu
from jax.sharding import PartitionSpec as P

RBLK = 32
NB = 2048
W = 128
NCOL = 16
NROW = 48
HALF = 64
META = 8
NT = (((1,), (1,)), ((), ()))
NN = (((1,), (0,)), ((), ()))
TN = (((0,), (0,)), ((), ()))
F32 = jnp.float32
BF16 = jnp.bfloat16
HIGH = lax.Precision.HIGHEST


def row_at(y_hi, z, core):
    return y_hi * 24 + z * 2 + core


CORES = [(r, r ^ 1) for r in range(NROW)]
PARTNERS = [(c, c ^ (NCOL // 2)) for c in range(NCOL)]


def sub(x, m):
    return jnp.broadcast_to(x[m : m + 1, :], x.shape)


def lane(x, m):
    return jnp.broadcast_to(x[:, m : m + 1], (8, W))


def cholesky_and_inverse(a):
    n = a.shape[0] // 8
    ri = lax.broadcasted_iota(jnp.int32, (8, W), 0)
    li = lax.broadcasted_iota(jnp.int32, (8, W), 1)
    rows = [a[8 * g : 8 * g + 8, :] for g in range(n)]
    inv_rows = [jnp.where(li == ri + 8 * g, 1.0, 0.0).astype(F32) for g in range(n)]
    upper, inverse = [], []
    for g in range(n):
        k = 8 * g
        ra, rb = rows[g], inv_rows[g]
        diag = [lane(ra, k + m) for m in range(8)]
        below = {h: [lane(rows[h], k + m) for m in range(8)] for h in range(g + 1, n)}
        ua, ub = ra, rb
        scale = jnp.zeros((8, W), F32)
        for m in range(8):
            r = lax.rsqrt(sub(diag[m], m))
            ba, bb = sub(ra, m), sub(rb, m)
            if m:
                ua = jnp.where(ri == m, ba, ua)
                ub = jnp.where(ri == m, bb, ub)
            scale = jnp.where(ri == m, r, scale)
            c = jnp.where(ri == m, 0.0, diag[m] * (r * r))
            for q in range(m + 1, 8):
                diag[q] = diag[q] - c * sub(diag[q], m)
            ra = ra - c * ba
            rb = rb - c * bb
        upper.append(jnp.where(li >= ri + k, ua * scale, 0.0))
        inverse.append(ub * scale)
        if g + 1 < n:
            qa, qb = ra * (scale * scale), rb * (scale * scale)
            sa = [sub(qa, m) for m in range(8)]
            sb = [sub(qb, m) for m in range(8)]
            for h in range(g + 1, n):
                for m in range(8):
                    rows[h] = rows[h] - below[h][m] * sa[m]
                    inv_rows[h] = inv_rows[h] - below[h][m] * sb[m]
    return jnp.concatenate(upper, 0), jnp.concatenate(inverse, 0)


def dot(a, b, dims, precision=None):
    return lax.dot_general(a, b, dims, precision=precision, preferred_element_type=F32)


FLAG, BLOCKS, CORE, PLACE = range(4)


def first_block(at, tile, out):
    count = at[0, BLOCKS] * RBLK
    live = lax.broadcasted_iota(jnp.int32, (NB, W), 1) < count
    u = jnp.where(live, tile[...].astype(F32), 0.0).astype(BF16)
    gram = dot(u, u, TN) / NB
    ri = lax.broadcasted_iota(jnp.int32, (W, W), 0)
    li = lax.broadcasted_iota(jnp.int32, (W, W), 1)
    gram = gram + jnp.where((ri == li) & (li >= count), 1.0, 0.0)
    upper, inverse = cholesky_and_inverse(gram)
    out[:W, :] = upper
    out[W : 2 * W, :] = inverse
    out[2 * W :, :] = jnp.full((8, W), count, jnp.int32).astype(F32)


def masked(at, near, far, first_near, first_far, here):
    swap = at[0, FLAG] == 1
    count = jnp.where(swap, first_far[2 * W : 2 * W + 1, :], first_near[2 * W : 2 * W + 1, :])
    tile = jnp.where(swap, far[here, :].astype(F32), near[here, :].astype(F32))
    live = lax.broadcasted_iota(jnp.int32, tile.shape, 1).astype(F32) < count
    return jnp.where(live, tile, 0.0).astype(BF16)


def own_rows(own, first):
    return jnp.concatenate([own[c, first : first + W, :] for c in range(NCOL)], 0)


def column_rows(at, first_half, second_half, whole):
    for core, ref in ((at[0, CORE], first_half), (1 - at[0, CORE], second_half)):
        for s in range(4):
            for q in range(4):
                block = 8 * (q // 2) + 2 * ((at[0, PLACE] + s) % 4) + q % 2
                start = pl.multiple_of(block * W + core * HALF, HALF)
                whole[pl.ds(start, HALF), :] = ref(s, q)


def couple(at, own, near, far, coupling, col_right):
    column_rows(at, lambda s, q: near[s, q, HALF:], lambda s, q: far[s, q, HALF:], col_right)
    coupling[...] = dot(own_rows(own, W), col_right[...], TN).astype(BF16)


def parts(x):
    high = x.astype(BF16)
    return high, (x - high.astype(F32)).astype(BF16)


def second_block(
    at, own, near, far, tile_near, tile_far, first_near, first_far, left_out, factor, lifted
):
    swap = at[0, FLAG] == 1
    coupling = jnp.where(swap, far[...].astype(F32), near[...].astype(F32)).astype(BF16)
    up = (-dot(own_rows(own, 0), coupling, NN)).astype(BF16)
    u = masked(at, tile_near, tile_far, first_near, first_far, pl.ds(0, NB))
    f11t = jnp.where(swap, first_far[:W, :], first_near[:W, :])
    inv11 = jnp.where(swap, first_far[W : 2 * W, :], first_near[W : 2 * W, :])
    g12 = dot(u, up, TN) / NB
    g22 = dot(up, up, TN) / NB
    f21t = dot(inv11, g12, NN, HIGH)
    f22t, inv22 = cholesky_and_inverse(g22 - dot(f21t, f21t, TN, HIGH))
    inv21 = -dot(inv22, dot(f21t, inv11, TN, HIGH), NN, HIGH)
    zero = jnp.zeros((W, W), F32)
    factor[...] = jnp.concatenate(
        [jnp.concatenate([f11t, f21t], 1), jnp.concatenate([zero, f22t], 1)], 0
    )
    inverse = jnp.concatenate(
        [jnp.concatenate([inv11, zero], 1), jnp.concatenate([inv21, inv22], 1)], 0
    )
    high, low = parts(inverse)
    lifted[...] = up
    for first in range(0, NB, 512):
        here = pl.ds(first, 512)
        rows = masked(at, tile_near, tile_far, first_near, first_far, here)
        s = jnp.concatenate([rows, lifted[here, :]], 1)
        left_out[here, :] = (dot(s, high, NT) + dot(s, low, NT)).astype(BF16)


def third_block(
    at, tile_near, tile_far, first_near, first_far, near, far, near_swapped, far_swapped, factor,
    right_out, col_left,
):
    flag = at[0, FLAG]

    def either(swapped, kept):
        def read(p, q):
            a, b = swapped[p, q].astype(F32), kept[p, q, :HALF].astype(F32)
            return jnp.where(flag == 1, a, b).astype(BF16)

        return read

    column_rows(at, either(near_swapped, near), either(far_swapped, far), col_left)
    high, low = parts(factor[...])
    for first in range(0, NB, 512):
        here = pl.ds(first, 512)
        v = masked(at, tile_near, tile_far, first_near, first_far, here)
        t = jnp.concatenate([v, col_left[here, :]], 1)
        right_out[here, :] = (dot(t, high, NT) + dot(t, low, NT)).astype(BF16)


VMEM = pl.BlockSpec(memory_space=pltpu.VMEM)
SMEM = pl.BlockSpec(memory_space=pltpu.SMEM)


def kernel(body, outs, scratch, megaflops, *args):
    return pl.pallas_call(
        body,
        out_shape=[jax.ShapeDtypeStruct(shape, dtype) for shape, dtype in outs],
        in_specs=[SMEM] + [VMEM] * (len(args) - 1),
        out_specs=[VMEM] * len(outs),
        scratch_shapes=[pltpu.VMEM((NB, W), BF16)] * scratch,
        compiler_params=pltpu.CompilerParams(vmem_limit_bytes=32 * 2**20),
        cost_estimate=pl.CostEstimate(
            flops=megaflops * 10**6, bytes_accessed=2**20, transcendentals=0
        ),
    )(*args)


def per_device(tile_left, tile_right, tile_blocks, panel_left, panel_right, swap_flag):
    row = lax.axis_index("row")
    col = lax.axis_index("col")
    core = row % 2

    blocks = jnp.concatenate(
        [panel_left[0].reshape(2, HALF, W), panel_right[0].reshape(2, HALF, W)], axis=1
    )
    even = col % 2 == 0
    turned = [
        lax.ppermute(
            jnp.where(even, blocks[k], blocks[1 - k]),
            ("row", "col"),
            [(j * NCOL + c, (c ^ k) * NCOL + j) for j in range(NCOL) for c in range(NCOL)],
        )
        for k in range(2)
    ]
    pair = jnp.where(core == 0, jnp.stack(turned), jnp.stack(turned[::-1]))

    at = jnp.stack([swap_flag[0, 0], tile_blocks[0, 0], core, (row // 2) % 4])
    at = at.astype(jnp.int32).reshape(1, 4)
    tile_left, tile_right = tile_left[0, 0], tile_right[0, 0]
    (first,) = kernel(first_block, [((2 * W + 8, W), F32)], 0, 6000, at, tile_left)
    pair, first = lax.optimization_barrier((pair, first))

    above = lax.ppermute(pair, "row", [(r, r + NROW // 2) for r in range(NCOL)])
    pair = jnp.where(row < NROW // 2, pair, above)
    sent = []
    for t in range(3):
        pairs = [
            (row_at(y, m, k), row_at(y, 4 * ((t + m // 4) % 3) + m % 4, k))
            for y in range(2)
            for m in range(8)
            for k in range(2)
        ]
        sent.append(lax.ppermute(pair, "row", pairs))
    first_far = lax.ppermute(first, "col", PARTNERS)
    tile_left_far = lax.ppermute(tile_left, "col", PARTNERS)
    tile_right_far = lax.ppermute(tile_right, "col", PARTNERS)
    sent, own_parts, first_far, tile_left_far, tile_right_far = lax.optimization_barrier(
        (sent, (panel_left[1, 0], panel_right[1, 0]), first_far, tile_left_far, tile_right_far)
    )
    run = (row % (NROW // 2)) // 8
    piece = jnp.concatenate(
        [
            jnp.where(run == 0, sent[0], jnp.where(run == 1, sent[1], sent[2])),
            jnp.where(run == 0, sent[2], jnp.where(run == 1, sent[0], sent[1])),
        ]
    )

    held = jnp.concatenate(own_parts, 0)
    own = lax.all_to_all(jnp.broadcast_to(held[None], (NCOL, 2 * W, W)), "col", 0, 0, tiled=True)
    near = [piece]
    for s in range(1, 4):
        pairs = [
            (row_at(y, 4 * g + (p + s) % 4, k), row_at(y, 4 * g + p, k))
            for y in range(2)
            for g in range(3)
            for p in range(4)
            for k in range(2)
        ]
        near.append(lax.ppermute(piece, "row", pairs))
    near = jnp.stack(near)
    near, own = lax.optimization_barrier((near, own))
    far = lax.ppermute(near, "row", CORES)
    near_swapped = lax.ppermute(near[:, :, :HALF], "col", PARTNERS)
    far_swapped = lax.ppermute(near_swapped, "row", CORES)

    (coupling,) = kernel(couple, [((W, W), BF16)], 1, 2000, at, own, near, far)
    coupling_far = lax.ppermute(coupling, "col", PARTNERS)
    left_out, factor = kernel(
        second_block, [((NB, 2 * W), BF16), ((2 * W, 2 * W), F32)], 1, 8000,
        at, own, coupling, coupling_far, tile_left, tile_left_far, first, first_far,
    )
    (right_out,) = kernel(
        third_block, [((NB, 2 * W), BF16)], 1, 2000,
        at, tile_right, tile_right_far, first, first_far, near, far, near_swapped, far_swapped, factor,
    )
    return left_out[None, None], right_out[None, None]


def solution(mesh):
    placed = (
        P("row", "col", None, None),
        P("row", "col", None, None),
        P("row", "col"),
        P(None, "row", "col", None),
        P(None, "row", "col", None),
        P("row", "col"),
    )
    return jax.shard_map(
        per_device,
        mesh=mesh,
        in_specs=placed,
        out_specs=(P("row", "col", None, None), P("row", "col", None, None)),
        check_vma=False,
    )
```

time: 138 us -> 119 us (0.86)
  waiting for transfers between devices: 37.1 us -> 24.6 us
  starting transfers between devices: 76.4 us -> 70.9 us
    all_to_all x2 -> x1, starting transfers between devices: 27.8 us -> 6.52 us  [per_device(): lax.all_to_all(jnp.broadcast_to(held[None], (NCOL, 2 * W, W)), 'col', 0,...]
    ppermute x7 -> x10, starting transfers between devices: 28.3 us -> 43.9 us  [the longest x2 16 us: per_device(): lax.ppermute(jnp.where(even, blocks[k], blocks[1 - k]), ('row', 'col'), [...]
    ppermute x1, waiting for transfers between devices: 8.51 us -> 0.01 us  [per_device(): tile_left_far = lax.ppermute(tile_left, 'col', PARTNERS)]
    all_to_all x2 -> x1, waiting for transfers between devices: 0.01 us -> 7.89 us  [per_device(): lax.all_to_all(jnp.broadcast_to(held[None], (NCOL, 2 * W, W)), 'col', 0,...]
    ppermute x7 -> x10, waiting for transfers between devices: 20.6 us -> 13.2 us  [the longest x3 7.63 us: per_device(): sent.append(lax.ppermute(pair, 'row', pairs))]
    ppermute x1, waiting for transfers between devices: 4.39 us -> 0.01 us  [per_device(): tile_right_far = lax.ppermute(tile_right, 'col', PARTNERS)]
  transfers between devices with their start and end apart: 15 -> 17, of which waited for: 8 -> 5; matrix products, arithmetic and copies ran while one was open for 0% -> 0% of each run, Pallas kernels for 11% -> 12%
where the time goes in v2:
time: 119 us; the launch traced here: 118 us
  starting transfers between devices  70.9 us (60%)
  waiting for transfers between devices  24.6 us (21%)
  Pallas kernels  16.8 us (14%)
  local copies, waits for them, and re-layouts  3.07 us (3%)
  between operations  2.33 us (2%)
    pallas_call x4, Pallas kernels, kernel(): pl.pallas_call(body, out_shape=[jax.ShapeDtypeStruct(shape, dtype) for sh...  16.8 us
    ppermute x2, starting transfers between devices, per_device(): lax.ppermute(jnp.where(even, blocks[k], blocks[1 - k]), ('row', 'col'), [...  16 us
    ppermute x3, starting transfers between devices, per_device(): near.append(lax.ppermute(piece, 'row', pairs))  13.3 us
    ppermute x3, starting transfers between devices, per_device(): sent.append(lax.ppermute(pair, 'row', pairs))  9.74 us
    all_to_all x1, waiting for transfers between devices, per_device(): lax.all_to_all(jnp.broadcast_to(held[None], (NCOL, 2 * W, W)), 'col', 0,...  7.89 us
    ppermute x3, waiting for transfers between devices, per_device(): sent.append(lax.ppermute(pair, 'row', pairs))  7.63 us
    all_to_all x1, starting transfers between devices, per_device(): lax.all_to_all(jnp.broadcast_to(held[None], (NCOL, 2 * W, W)), 'col', 0,...  6.52 us
    ppermute x3, waiting for transfers between devices, per_device(): near.append(lax.ppermute(piece, 'row', pairs))  5.6 us
  transfers between devices with their start and end apart: 17, of which 5 were waited for; matrix products, arithmetic and copies ran while one was open for 0% of the time, Pallas kernels for 12%

profile of v2, /device:TPU:1, one launch (start us, length us, event | category | flops | bytes accessed | tf_op | source)
XLA Modules:
  0.0 118.0 jit_solution(13365755172717271675)
XLA Ops:
  0.6 0.8 slice_bitcast_fusion
  1.5 4.0 %collective-permute-start.1 = (bf16[128,128]{1,0:T(8,128)(2,1)S(1)}, bf16[128,128]{1,0:T(8,128)(2,1)S(1)}, u32[]{:S(2)}, u32[]{:S(2)}) collective-permute-start(bf16[128,128]{1,0:T(8,128)(2,1)S(1)} %get-tuple-element.39), channel_id=1, source_target_pairs={{0,16},{1,0},{2,48},{3,32},{4,80},{5,64},{6,112},{7,96},{8,144},{9... | collective-permute-start | bytes 98312 | tf_op jit(solution)/shard_map/ppermute | solution.py:210
  5.5 11.9 %collective-permute-start = (bf16[128,128]{1,0:T(8,128)(2,1)S(1)}, bf16[128,128]{1,0:T(8,128)(2,1)S(1)}, u32[]{:S(2)}, u32[]{:S(2)}) collective-permute-start(bf16[128,128]{1,0:T(8,128)(2,1)S(1)} %get-tuple-element.38), channel_id=1, source_target_pairs={{0,0},{1,16},{2,32},{3,48},{4,64},{5,80},{6,96},{7,112},{8,128},{9... | collective-permute-start | bytes 98312 | tf_op jit(solution)/shard_map/ppermute | solution.py:210
  17.5 3.6 %collective-permute-start.7 = (bf16[2048,128]{1,0:T(8,128)(2,1)}, bf16[2048,128]{1,0:T(8,128)(2,1)S(1)}, u32[]{:S(2)}, u32[]{:S(2)}) collective-permute-start(bf16[2048,128]{1,0:T(8,128)(2,1)} %bitcast.29), channel_id=1, source_target_pairs={{0,8},{1,9},{2,10},{3,11},{4,12},{5,13},{6,14},{7,15},{8,0},{9,1},... | collective-permute-start | bytes 1572872 | tf_op jit(solution)/shard_map/ppermute | solution.py:237
  21.1 3.2 %collective-permute-start.8 = (bf16[2048,128]{1,0:T(8,128)(2,1)}, bf16[2048,128]{1,0:T(8,128)(2,1)S(1)}, u32[]{:S(2)}, u32[]{:S(2)}) collective-permute-start(bf16[2048,128]{1,0:T(8,128)(2,1)} %bitcast.32), channel_id=1, source_target_pairs={{0,8},{1,9},{2,10},{3,11},{4,12},{5,13},{6,14},{7,15},{8,0},{9,1},... | collective-permute-start | bytes 1572872 | tf_op jit(solution)/shard_map/ppermute | solution.py:238
  25.6 0.1 add_bitcast_fusion.at
  25.7 0.0 copy-start
  25.7 1.0 copy-done
  26.7 5.4 %shard_map.77.first_near = f32[264,128]{1,0:T(8,128)S(1)} custom-call(s32[1,4]{1,0:T(1,128)S(1)} %add_bitcast_fusion.at, bf16[2048,128]{1,0:T(8,128)(2,1)S(1)} %bitcast.30), custom_call_target="tpu_custom_call" | custom-call | flops 6000000000 | bytes 1048576 | tf_op jit(solution)/shard_map/pallas_call | solution.py:187
  32.1 0.0 collective-permute-done.1
  32.2 0.0 collective-permute-done
  32.2 1.3 %collective-permute-start.2 = (bf16[2,128,128]{2,1,0:T(8,128)(2,1)S(1)}, bf16[2,128,128]{2,1,0:T(8,128)(2,1)S(1)}, u32[]{:S(2)}, u32[]{:S(2)}) collective-permute-start(bf16[2,128,128]{2,1,0:T(8,128)(2,1)S(1)} %maximum_select_fusion), channel_id=1, source_target_pairs={{0,384},{16,400},{32,416},{48,432},{64,448},{80,464},{96,480},{112... | collective-permute-start | bytes 196616 | tf_op jit(solution)/shard_map/ppermute | solution.py:225
  33.5 3.6 %collective-permute-start.6 = (f32[264,128]{1,0:T(8,128)S(1)}, f32[264,128]{1,0:T(8,128)S(1)}, u32[]{:S(2)}, u32[]{:S(2)}) collective-permute-start(f32[264,128]{1,0:T(8,128)S(1)} %shard_map.77.first_near), channel_id=1, source_target_pairs={{0,8},{1,9},{2,10},{3,11},{4,12},{5,13},{6,14},{7,15},{8,0},{9,1},... | collective-permute-start | bytes 405512 | tf_op jit(solution)/shard_map/ppermute | solution.py:236
  37.1 0.0 collective-permute-done.2
  37.1 0.7 collective-permute-start.3
  37.8 7.2 %collective-permute-start.4 = (bf16[2,128,128]{2,1,0:T(8,128)(2,1)S(1)}, bf16[2,128,128]{2,1,0:T(8,128)(2,1)S(1)}, u32[]{:S(2)}, u32[]{:S(2)}) collective-permute-start(bf16[2,128,128]{2,1,0:T(8,128)(2,1)S(1)} %broadcast_select_fusion), channel_id=1, source_target_pairs={{0,128},{16,144},{32,160},{48,176},{64,192},{80,208},{96,224},{112... | collective-permute-start | bytes 196616 | tf_op jit(solution)/shard_map/ppermute | solution.py:235
  45.0 0.0 collective-permute-done.3
  45.0 1.9 %collective-permute-start.5 = (bf16[2,128,128]{2,1,0:T(8,128)(2,1)S(1)}, bf16[2,128,128]{2,1,0:T(8,128)(2,1)S(1)}, u32[]{:S(2)}, u32[]{:S(2)}) collective-permute-start(bf16[2,128,128]{2,1,0:T(8,128)(2,1)S(1)} %broadcast_select_fusion), channel_id=1, source_target_pairs={{0,256},{16,272},{32,288},{48,304},{64,320},{80,336},{96,352},{112... | collective-permute-start | bytes 196616 | tf_op jit(solution)/shard_map/ppermute | solution.py:235
  46.9 0.0 collective-permute-done.4
  46.9 7.6 %collective-permute-done.5 = bf16[2,128,128]{2,1,0:T(8,128)(2,1)S(1)} collective-permute-done((bf16[2,128,128]{2,1,0:T(8,128)(2,1)S(1)}, bf16[2,128,128]{2,1,0:T(8,128)(2,1)S(1)}, u32[]{:S(2)}, u32[]{:S(2)}) %collective-permute-start.5) | collective-permute-done | bytes 65568 | tf_op jit(solution)/shard_map/ppermute | solution.py:235
  54.5 0.0 collective-permute-done.6.first_far
  54.5 0.0 collective-permute-done.7.tile_far
  54.5 0.0 collective-permute-done.8.tile_far
  54.6 1.2 broadcast_in_dim.12
  55.7 6.5 %all-to-all-start = ((bf16[16,256,128]{2,1,0:T(8,128)(2,1)}), bf16[16,256,128]{2,1,0:T(8,128)(2,1)S(1)}, u32[]{:S(2)}, u32[]{:S(2)}) async-start(bf16[16,256,128]{2,1,0:T(8,128)(2,1)} %broadcast_in_dim.12), calls=%async_computation | async-start | bytes 2097152 | tf_op jit(solution)/shard_map/all_to_all | solution.py:251
  62.3 9.2 %collective-permute-start.9 = (bf16[4,128,128]{2,1,0:T(8,128)(2,1)S(1)}, bf16[4,128,128]{2,1,0:T(8,128)(2,1)S(1)}, u32[]{:S(2)}, u32[]{:S(2)}) collective-permute-start(bf16[4,128,128]{2,1,0:T(8,128)(2,1)S(1)} %get-tuple-element.33), channel_id=1, source_target_pairs={{32,0},{48,16},{64,32},{80,48},{96,64},{112,80},{0,96},{16,112},{1... | collective-permute-start | bytes 393224 | tf_op jit(solution)/shard_map/ppermute | solution.py:261
  71.5 1.9 %collective-permute-start.10 = (bf16[4,128,128]{2,1,0:T(8,128)(2,1)S(1)}, bf16[4,128,128]{2,1,0:T(8,128)(2,1)S(1)}, u32[]{:S(2)}, u32[]{:S(2)}) collective-permute-start(bf16[4,128,128]{2,1,0:T(8,128)(2,1)S(1)} %get-tuple-element.33), channel_id=1, source_target_pairs={{64,0},{80,16},{96,32},{112,48},{0,64},{16,80},{32,96},{48,112},{1... | collective-permute-start | bytes 393224 | tf_op jit(solution)/shard_map/ppermute | solution.py:261
  73.5 2.2 %collective-permute-start.11 = (bf16[4,128,128]{2,1,0:T(8,128)(2,1)S(1)}, bf16[4,128,128]{2,1,0:T(8,128)(2,1)S(1)}, u32[]{:S(2)}, u32[]{:S(2)}) collective-permute-start(bf16[4,128,128]{2,1,0:T(8,128)(2,1)S(1)} %get-tuple-element.33), channel_id=1, source_target_pairs={{96,0},{112,16},{0,32},{16,48},{32,64},{48,80},{64,96},{80,112},{2... | collective-permute-start | bytes 393224 | tf_op jit(solution)/shard_map/ppermute | solution.py:261
  75.7 0.0 collective-permute-done.9
  75.7 4.2 %collective-permute-done.10 = bf16[4,128,128]{2,1,0:T(8,128)(2,1)S(1)} collective-permute-done((bf16[4,128,128]{2,1,0:T(8,128)(2,1)S(1)}, bf16[4,128,128]{2,1,0:T(8,128)(2,1)S(1)}, u32[]{:S(2)}, u32[]{:S(2)}) %collective-permute-start.10) | collective-permute-done | bytes 131104 | tf_op jit(solution)/shard_map/ppermute | solution.py:261
  79.9 1.4 %collective-permute-done.11 = bf16[4,128,128]{2,1,0:T(8,128)(2,1)S(1)} collective-permute-done((bf16[4,128,128]{2,1,0:T(8,128)(2,1)S(1)}, bf16[4,128,128]{2,1,0:T(8,128)(2,1)S(1)}, u32[]{:S(2)}, u32[]{:S(2)}) %collective-permute-start.11) | collective-permute-done | bytes 131104 | tf_op jit(solution)/shard_map/ppermute | solution.py:261
  81.3 0.1 pad_maximum_fusion.near
  81.3 7.9 %all-to-all-done.own = bf16[16,256,128]{2,1,0:T(8,128)(2,1)S(1)} async-done(((bf16[16,256,128]{2,1,0:T(8,128)(2,1)}), bf16[16,256,128]{2,1,0:T(8,128)(2,1)S(1)}, u32[]{:S(2)}, u32[]{:S(2)}) %all-to-all-start) | async-done | bytes 1048608 | tf_op jit(solution)/shard_map/all_to_all | solution.py:251
  89.2 3.7 %collective-permute-start.12 = (bf16[4,4,128,128]{3,2,1,0:T(8,128)(2,1)S(1)}, bf16[4,4,128,128]{3,2,1,0:T(8,128)(2,1)S(1)}, u32[]{:S(2)}, u32[]{:S(2)}) collective-permute-start(bf16[4,4,128,128]{3,2,1,0:T(8,128)(2,1)S(1)} %pad_maximum_fusion.near), channel_id=1, source_target_pairs={{0,16},{16,0},{32,48},{48,32},{64,80},{80,64},{96,112},{112,96},{1... | collective-permute-start | bytes 1572872 | tf_op jit(solution)/shard_map/ppermute | solution.py:264
  92.9 0.0 copy-start.1
  92.9 2.6 %collective-permute-start.14 = (bf16[4,4,64,128]{3,2,1,0:T(8,128)(2,1)S(1)}, bf16[4,4,64,128]{3,2,1,0:T(8,128)(2,1)S(1)}, u32[]{:S(2)}, u32[]{:S(2)}) collective-permute-start(bf16[4,4,64,128]{3,2,1,0:T(8,128)(2,1)S(1)} %slice.29), channel_id=1, source_target_pairs={{0,8},{1,9},{2,10},{3,11},{4,12},{5,13},{6,14},{7,15},{8,0},{9,1},... | collective-permute-start | bytes 786440 | tf_op jit(solution)/shard_map/ppermute | solution.py:265
  95.6 0.0 collective-permute-done.12.far
  95.6 0.9 shard_map.78.near
  96.5 0.0 copy-start.2
  96.5 4.4 %collective-permute-start.13 = (bf16[128,128]{1,0:T(8,128)(2,1)S(1)}, bf16[128,128]{1,0:T(8,128)(2,1)S(1)}, u32[]{:S(2)}, u32[]{:S(2)}) collective-permute-start(bf16[128,128]{1,0:T(8,128)(2,1)S(1)} %shard_map.78.near), channel_id=1, source_target_pairs={{0,8},{1,9},{2,10},{3,11},{4,12},{5,13},{6,14},{7,15},{8,0},{9,1},... | collective-permute-start | bytes 98312 | tf_op jit(solution)/shard_map/ppermute | solution.py:269
  101.0 3.4 %collective-permute-done.14.near_swapped = bf16[4,4,64,128]{3,2,1,0:T(8,128)(2,1)S(1)} collective-permute-done((bf16[4,4,64,128]{3,2,1,0:T(8,128)(2,1)S(1)}, bf16[4,4,64,128]{3,2,1,0:T(8,128)(2,1)S(1)}, u32[]{:S(2)}, u32[]{:S(2)}) %collective-permute-start.14) | collective-permute-done | bytes 262176 | tf_op jit(solution)/shard_map/ppermute | solution.py:265
  104.4 3.0 %collective-permute-start.15 = (bf16[4,4,64,128]{3,2,1,0:T(8,128)(2,1)S(1)}, bf16[4,4,64,128]{3,2,1,0:T(8,128)(2,1)S(1)}, u32[]{:S(2)}, u32[]{:S(2)}) collective-permute-start(bf16[4,4,64,128]{3,2,1,0:T(8,128)(2,1)S(1)} %collective-permute-done.14.near_swapped), channel_id=1, source_target_pairs={{0,16},{16,0},{32,48},{48,32},{64,80},{80,64},{96,112},{112,96},{1... | collective-permute-start | bytes 786440 | tf_op jit(solution)/shard_map/ppermute | solution.py:266
  107.4 0.0 collective-permute-done.13.far
  107.5 0.0 copy-done.1
  107.5 8.2 %shard_map.79 = (bf16[2048,256]{1,0:T(8,128)(2,1)}, f32[256,256]{1,0:T(8,128)S(1)}) custom-call(s32[1,4]{1,0:T(1,128)S(1)} %add_bitcast_fusion.at, bf16[16,256,128]{2,1,0:T(8,128)(2,1)S(1)} %all-to-all-done.own, bf16[128,128]{1,0:T(8,128)(2,1)S(1)} %shard_map.78.near, bf16[128,128]{1,0:T(8,128)(2,1)S(1)} %collective-permute-done.13.far, ...), custom_call_target="tpu_custom_call" | custom-call | flops 8000000000 | bytes 1048576 | tf_op jit(solution)/shard_map/pallas_call | solution.py:187
  115.6 0.0 collective-permute-done.15.far_swapped
  115.6 0.0 copy-done.2
  115.6 2.3 %shard_map.80 = bf16[2048,256]{1,0:T(8,128)(2,1)} custom-call(s32[1,4]{1,0:T(1,128)S(1)} %add_bitcast_fusion.at, bf16[2048,128]{1,0:T(8,128)(2,1)S(1)} %bitcast.33, bf16[2048,128]{1,0:T(8,128)(2,1)S(1)} %collective-permute-done.8.tile_far, f32[264,128]{1,0:T(8,128)S(1)} %shard_map.77.first_near, f32[264,128]{1,0:T(8,128)S(1)} %collective-permute-done.6.first_far, ...), custom_call_target="tpu_custom_call" | custom-call | flops 2000000000 | bytes 1048576 | tf_op jit(solution)/shard_map/pallas_call | solution.py:187
  (7 shorter events, 0.1 us)
Async XLA Ops:
  1.5 30.7 %collective-permute-start.1 = (bf16[128,128]{1,0:T(8,128)(2,1)S(1)}, bf16[128,128]{1,0:T(8,128)(2,1)S(1)}, u32[]{:S(2)}, u32[]{:S(2)}) collective-permute-start(bf16[128,128]{1,0:T(8,128)(2,1)S(1)} %get-tuple-element.39), channel_id=1, source_target_pairs={{0,16},{1,0},{2,48},{3,32},{4,80},{5,64},{6,112},{7,96},{8,144},{9... | collective-permute-start | bytes 98312 | tf_op jit(solution)/shard_map/ppermute | solution.py:210
  5.5 26.6 %collective-permute-start = (bf16[128,128]{1,0:T(8,128)(2,1)S(1)}, bf16[128,128]{1,0:T(8,128)(2,1)S(1)}, u32[]{:S(2)}, u32[]{:S(2)}) collective-permute-start(bf16[128,128]{1,0:T(8,128)(2,1)S(1)} %get-tuple-element.38), channel_id=1, source_target_pairs={{0,0},{1,16},{2,32},{3,48},{4,64},{5,80},{6,96},{7,112},{8,128},{9... | collective-permute-start | bytes 98312 | tf_op jit(solution)/shard_map/ppermute | solution.py:210
  17.5 37.1 %collective-permute-start.7 = (bf16[2048,128]{1,0:T(8,128)(2,1)}, bf16[2048,128]{1,0:T(8,128)(2,1)S(1)}, u32[]{:S(2)}, u32[]{:S(2)}) collective-permute-start(bf16[2048,128]{1,0:T(8,128)(2,1)} %bitcast.29), channel_id=1, source_target_pairs={{0,8},{1,9},{2,10},{3,11},{4,12},{5,13},{6,14},{7,15},{8,0},{9,1},... | collective-permute-start | bytes 1572872 | tf_op jit(solution)/shard_map/ppermute | solution.py:237
  21.1 33.5 %collective-permute-start.8 = (bf16[2048,128]{1,0:T(8,128)(2,1)}, bf16[2048,128]{1,0:T(8,128)(2,1)S(1)}, u32[]{:S(2)}, u32[]{:S(2)}) collective-permute-start(bf16[2048,128]{1,0:T(8,128)(2,1)} %bitcast.32), channel_id=1, source_target_pairs={{0,8},{1,9},{2,10},{3,11},{4,12},{5,13},{6,14},{7,15},{8,0},{9,1},... | collective-permute-start | bytes 1572872 | tf_op jit(solution)/shard_map/ppermute | solution.py:238
  25.7 1.0 copy-start
  32.2 4.9 %collective-permute-start.2 = (bf16[2,128,128]{2,1,0:T(8,128)(2,1)S(1)}, bf16[2,128,128]{2,1,0:T(8,128)(2,1)S(1)}, u32[]{:S(2)}, u32[]{:S(2)}) collective-permute-start(bf16[2,128,128]{2,1,0:T(8,128)(2,1)S(1)} %maximum_select_fusion), channel_id=1, source_target_pairs={{0,384},{16,400},{32,416},{48,432},{64,448},{80,464},{96,480},{112... | collective-permute-start | bytes 196616 | tf_op jit(solution)/shard_map/ppermute | solution.py:225
  33.5 21.0 %collective-permute-start.6 = (f32[264,128]{1,0:T(8,128)S(1)}, f32[264,128]{1,0:T(8,128)S(1)}, u32[]{:S(2)}, u32[]{:S(2)}) collective-permute-start(f32[264,128]{1,0:T(8,128)S(1)} %shard_map.77.first_near), channel_id=1, source_target_pairs={{0,8},{1,9},{2,10},{3,11},{4,12},{5,13},{6,14},{7,15},{8,0},{9,1},... | collective-permute-start | bytes 405512 | tf_op jit(solution)/shard_map/ppermute | solution.py:236
  37.1 7.8 %collective-permute-start.3 = (bf16[2,128,128]{2,1,0:T(8,128)(2,1)S(1)}, bf16[2,128,128]{2,1,0:T(8,128)(2,1)S(1)}, u32[]{:S(2)}, u32[]{:S(2)}) collective-permute-start(bf16[2,128,128]{2,1,0:T(8,128)(2,1)S(1)} %broadcast_select_fusion), channel_id=1, source_target_pairs={{0,0},{16,16},{32,32},{48,48},{64,64},{80,80},{96,96},{112,112},{1... | collective-permute-start | bytes 196616 | tf_op jit(solution)/shard_map/ppermute | solution.py:235
  37.8 9.1 %collective-permute-start.4 = (bf16[2,128,128]{2,1,0:T(8,128)(2,1)S(1)}, bf16[2,128,128]{2,1,0:T(8,128)(2,1)S(1)}, u32[]{:S(2)}, u32[]{:S(2)}) collective-permute-start(bf16[2,128,128]{2,1,0:T(8,128)(2,1)S(1)} %broadcast_select_fusion), channel_id=1, source_target_pairs={{0,128},{16,144},{32,160},{48,176},{64,192},{80,208},{96,224},{112... | collective-permute-start | bytes 196616 | tf_op jit(solution)/shard_map/ppermute | solution.py:235
  45.0 9.6 %collective-permute-start.5 = (bf16[2,128,128]{2,1,0:T(8,128)(2,1)S(1)}, bf16[2,128,128]{2,1,0:T(8,128)(2,1)S(1)}, u32[]{:S(2)}, u32[]{:S(2)}) collective-permute-start(bf16[2,128,128]{2,1,0:T(8,128)(2,1)S(1)} %broadcast_select_fusion), channel_id=1, source_target_pairs={{0,256},{16,272},{32,288},{48,304},{64,320},{80,336},{96,352},{112... | collective-permute-start | bytes 196616 | tf_op jit(solution)/shard_map/ppermute | solution.py:235
  55.7 33.5 %all-to-all-start = ((bf16[16,256,128]{2,1,0:T(8,128)(2,1)}), bf16[16,256,128]{2,1,0:T(8,128)(2,1)S(1)}, u32[]{:S(2)}, u32[]{:S(2)}) async-start(bf16[16,256,128]{2,1,0:T(8,128)(2,1)} %broadcast_in_dim.12), calls=%async_computation | async-start | bytes 2097152 | tf_op jit(solution)/shard_map/all_to_all | solution.py:251
  62.3 13.3 %collective-permute-start.9 = (bf16[4,128,128]{2,1,0:T(8,128)(2,1)S(1)}, bf16[4,128,128]{2,1,0:T(8,128)(2,1)S(1)}, u32[]{:S(2)}, u32[]{:S(2)}) collective-permute-start(bf16[4,128,128]{2,1,0:T(8,128)(2,1)S(1)} %get-tuple-element.33), channel_id=1, source_target_pairs={{32,0},{48,16},{64,32},{80,48},{96,64},{112,80},{0,96},{16,112},{1... | collective-permute-start | bytes 393224 | tf_op jit(solution)/shard_map/ppermute | solution.py:261
  71.5 8.4 %collective-permute-start.10 = (bf16[4,128,128]{2,1,0:T(8,128)(2,1)S(1)}, bf16[4,128,128]{2,1,0:T(8,128)(2,1)S(1)}, u32[]{:S(2)}, u32[]{:S(2)}) collective-permute-start(bf16[4,128,128]{2,1,0:T(8,128)(2,1)S(1)} %get-tuple-element.33), channel_id=1, source_target_pairs={{64,0},{80,16},{96,32},{112,48},{0,64},{16,80},{32,96},{48,112},{1... | collective-permute-start | bytes 393224 | tf_op jit(solution)/shard_map/ppermute | solution.py:261
  73.5 7.8 %collective-permute-start.11 = (bf16[4,128,128]{2,1,0:T(8,128)(2,1)S(1)}, bf16[4,128,128]{2,1,0:T(8,128)(2,1)S(1)}, u32[]{:S(2)}, u32[]{:S(2)}) collective-permute-start(bf16[4,128,128]{2,1,0:T(8,128)(2,1)S(1)} %get-tuple-element.33), channel_id=1, source_target_pairs={{96,0},{112,16},{0,32},{16,48},{32,64},{48,80},{64,96},{80,112},{2... | collective-permute-start | bytes 393224 | tf_op jit(solution)/shard_map/ppermute | solution.py:261
  89.2 6.3 %collective-permute-start.12 = (bf16[4,4,128,128]{3,2,1,0:T(8,128)(2,1)S(1)}, bf16[4,4,128,128]{3,2,1,0:T(8,128)(2,1)S(1)}, u32[]{:S(2)}, u32[]{:S(2)}) collective-permute-start(bf16[4,4,128,128]{3,2,1,0:T(8,128)(2,1)S(1)} %pad_maximum_fusion.near), channel_id=1, source_target_pairs={{0,16},{16,0},{32,48},{48,32},{64,80},{80,64},{96,112},{112,96},{1... | collective-permute-start | bytes 1572872 | tf_op jit(solution)/shard_map/ppermute | solution.py:264
  92.9 14.5 %copy-start.1 = (bf16[1,1,2048,128]{3,2,1,0:T(8,128)(2,1)S(1)}, bf16[1,1,2048,128]{3,2,1,0:T(8,128)(2,1)}, u32[]{:S(2)}) copy-start(bf16[1,1,2048,128]{3,2,1,0:T(8,128)(2,1)} %param.6) | copy-start | bytes 1572868
  92.9 11.5 %collective-permute-start.14 = (bf16[4,4,64,128]{3,2,1,0:T(8,128)(2,1)S(1)}, bf16[4,4,64,128]{3,2,1,0:T(8,128)(2,1)S(1)}, u32[]{:S(2)}, u32[]{:S(2)}) collective-permute-start(bf16[4,4,64,128]{3,2,1,0:T(8,128)(2,1)S(1)} %slice.29), channel_id=1, source_target_pairs={{0,8},{1,9},{2,10},{3,11},{4,12},{5,13},{6,14},{7,15},{8,0},{9,1},... | collective-permute-start | bytes 786440 | tf_op jit(solution)/shard_map/ppermute | solution.py:265
  96.5 19.1 %copy-start.2 = (bf16[1,1,2048,128]{3,2,1,0:T(8,128)(2,1)S(1)}, bf16[1,1,2048,128]{3,2,1,0:T(8,128)(2,1)}, u32[]{:S(2)}) copy-start(bf16[1,1,2048,128]{3,2,1,0:T(8,128)(2,1)} %param.7) | copy-start | bytes 1572868
  96.5 10.9 %collective-permute-start.13 = (bf16[128,128]{1,0:T(8,128)(2,1)S(1)}, bf16[128,128]{1,0:T(8,128)(2,1)S(1)}, u32[]{:S(2)}, u32[]{:S(2)}) collective-permute-start(bf16[128,128]{1,0:T(8,128)(2,1)S(1)} %shard_map.78.near), channel_id=1, source_target_pairs={{0,8},{1,9},{2,10},{3,11},{4,12},{5,13},{6,14},{7,15},{8,0},{9,1},... | collective-permute-start | bytes 98312 | tf_op jit(solution)/shard_map/ppermute | solution.py:269
  104.4 11.2 %collective-permute-start.15 = (bf16[4,4,64,128]{3,2,1,0:T(8,128)(2,1)S(1)}, bf16[4,4,64,128]{3,2,1,0:T(8,128)(2,1)S(1)}, u32[]{:S(2)}, u32[]{:S(2)}) collective-permute-start(bf16[4,4,64,128]{3,2,1,0:T(8,128)(2,1)S(1)} %collective-permute-done.14.near_swapped), channel_id=1, source_target_pairs={{0,16},{16,0},{32,48},{48,32},{64,80},{80,64},{96,112},{112,96},{1... | collective-permute-start | bytes 786440 | tf_op jit(solution)/shard_map/ppermute | solution.py:266

commit v3 on v2

--- a/solution.py
+++ b/solution.py
@@ -234,10 +234,9 @@
         ]
         sent.append(lax.ppermute(pair, "row", pairs))
     first_far = lax.ppermute(first, "col", PARTNERS)
-    tile_left_far = lax.ppermute(tile_left, "col", PARTNERS)
     tile_right_far = lax.ppermute(tile_right, "col", PARTNERS)
-    sent, own_parts, first_far, tile_left_far, tile_right_far = lax.optimization_barrier(
-        (sent, (panel_left[1, 0], panel_right[1, 0]), first_far, tile_left_far, tile_right_far)
+    sent, own_parts, tile_swap, first_far, tile_right_far = lax.optimization_barrier(
+        (sent, (panel_left[1, 0], panel_right[1, 0]), tile_left, first_far, tile_right_far)
     )
     run = (row % (NROW // 2)) // 8
     piece = jnp.concatenate(
@@ -249,6 +248,7 @@
 
     held = jnp.concatenate(own_parts, 0)
     own = lax.all_to_all(jnp.broadcast_to(held[None], (NCOL, 2 * W, W)), "col", 0, 0, tiled=True)
+    tile_left_far = lax.ppermute(tile_swap, "col", PARTNERS)
     near = [piece]
     for s in range(1, 4):
         pairs = [
@@ -260,7 +260,7 @@
         ]
         near.append(lax.ppermute(piece, "row", pairs))
     near = jnp.stack(near)
-    near, own = lax.optimization_barrier((near, own))
+    near, own, tile_left_far = lax.optimization_barrier((near, own, tile_left_far))
     far = lax.ppermute(near, "row", CORES)
     near_swapped = lax.ppermute(near[:, :, :HALF], "col", PARTNERS)
     far_swapped = lax.ppermute(near_swapped, "row", CORES)

time: 119 us -> 116 us (0.975)
  the two profiles are of different devices: /device:TPU:1 before, /device:TPU:193 now
where the time goes in v3:
time: 116 us
  starting transfers between devices  69 us (59%)
  waiting for transfers between devices  24.3 us (21%)
  Pallas kernels  16.9 us (15%)
  local copies, waits for them, and re-layouts  3.07 us (3%)
  between operations  2.31 us (2%)
    ppermute x3, starting transfers between devices, per_device(): sent.append(lax.ppermute(pair, 'row', pairs))  18.3 us
    pallas_call x4, Pallas kernels, kernel(): pl.pallas_call(body, out_shape=[jax.ShapeDtypeStruct(shape, dtype) for sh...  16.9 us
    ppermute x2, starting transfers between devices, per_device(): lax.ppermute(jnp.where(even, blocks[k], blocks[1 - k]), ('row', 'col'), [...  11.5 us
    ppermute x3, starting transfers between devices, per_device(): near.append(lax.ppermute(piece, 'row', pairs))  9 us
    ppermute x3, waiting for transfers between devices, per_device(): sent.append(lax.ppermute(pair, 'row', pairs))  7.74 us
    ppermute x3, waiting for transfers between devices, per_device(): near.append(lax.ppermute(piece, 'row', pairs))  5.54 us
    ppermute x1, waiting for transfers between devices, per_device(): tile_left_far = lax.ppermute(tile_swap, 'col', PARTNERS)  4.87 us
    ppermute x1, starting transfers between devices, per_device(): tile_left_far = lax.ppermute(tile_swap, 'col', PARTNERS)  4.66 us
  transfers between devices with their start and end apart: 17, of which 6 were waited for; matrix products, arithmetic and copies ran while one was open for 0% of the time, Pallas kernels for 13%

profile of v3, /device:TPU:193, one launch (start us, length us, event | category | flops | bytes accessed | tf_op | source)
XLA Modules:
  0.0 115.7 jit_solution(5321368674551635813)
XLA Ops:
  0.6 0.8 slice_bitcast_fusion
  1.5 3.4 %collective-permute-start.1 = (bf16[128,128]{1,0:T(8,128)(2,1)S(1)}, bf16[128,128]{1,0:T(8,128)(2,1)S(1)}, u32[]{:S(2)}, u32[]{:S(2)}) collective-permute-start(bf16[128,128]{1,0:T(8,128)(2,1)S(1)} %get-tuple-element.41), channel_id=1, source_target_pairs={{0,16},{1,0},{2,48},{3,32},{4,80},{5,64},{6,112},{7,96},{8,144},{9... | collective-permute-start | bytes 98312 | tf_op jit(solution)/shard_map/ppermute | solution.py:210
  4.9 8.1 %collective-permute-start = (bf16[128,128]{1,0:T(8,128)(2,1)S(1)}, bf16[128,128]{1,0:T(8,128)(2,1)S(1)}, u32[]{:S(2)}, u32[]{:S(2)}) collective-permute-start(bf16[128,128]{1,0:T(8,128)(2,1)S(1)} %get-tuple-element.40), channel_id=1, source_target_pairs={{0,0},{1,16},{2,32},{3,48},{4,64},{5,80},{6,96},{7,112},{8,128},{9... | collective-permute-start | bytes 98312 | tf_op jit(solution)/shard_map/ppermute | solution.py:210
  13.0 4.1 %collective-permute-start.7 = (bf16[2048,128]{1,0:T(8,128)(2,1)}, bf16[2048,128]{1,0:T(8,128)(2,1)S(1)}, u32[]{:S(2)}, u32[]{:S(2)}) collective-permute-start(bf16[2048,128]{1,0:T(8,128)(2,1)} %bitcast.32), channel_id=1, source_target_pairs={{0,8},{1,9},{2,10},{3,11},{4,12},{5,13},{6,14},{7,15},{8,0},{9,1},... | collective-permute-start | bytes 1572872 | tf_op jit(solution)/shard_map/ppermute | solution.py:237
  18.4 0.1 add_bitcast_fusion.at
  18.5 0.0 copy-start
  18.5 1.0 copy-done
  19.6 5.4 %shard_map.77.first_near = f32[264,128]{1,0:T(8,128)S(1)} custom-call(s32[1,4]{1,0:T(1,128)S(1)} %add_bitcast_fusion.at, bf16[2048,128]{1,0:T(8,128)(2,1)S(1)} %bitcast.29), custom_call_target="tpu_custom_call" | custom-call | flops 6000000000 | bytes 1048576 | tf_op jit(solution)/shard_map/pallas_call | solution.py:187
  25.0 0.0 collective-permute-done.1
  25.0 0.0 collective-permute-done
  25.0 1.3 %collective-permute-start.2 = (bf16[2,128,128]{2,1,0:T(8,128)(2,1)S(1)}, bf16[2,128,128]{2,1,0:T(8,128)(2,1)S(1)}, u32[]{:S(2)}, u32[]{:S(2)}) collective-permute-start(bf16[2,128,128]{2,1,0:T(8,128)(2,1)S(1)} %maximum_select_fusion), channel_id=1, source_target_pairs={{0,384},{16,400},{32,416},{48,432},{64,448},{80,464},{96,480},{112... | collective-permute-start | bytes 196616 | tf_op jit(solution)/shard_map/ppermute | solution.py:225
  26.3 2.7 %collective-permute-start.6 = (f32[264,128]{1,0:T(8,128)S(1)}, f32[264,128]{1,0:T(8,128)S(1)}, u32[]{:S(2)}, u32[]{:S(2)}) collective-permute-start(f32[264,128]{1,0:T(8,128)S(1)} %shard_map.77.first_near), channel_id=1, source_target_pairs={{0,8},{1,9},{2,10},{3,11},{4,12},{5,13},{6,14},{7,15},{8,0},{9,1},... | collective-permute-start | bytes 405512 | tf_op jit(solution)/shard_map/ppermute | solution.py:236
  29.0 0.0 collective-permute-done.2
  29.1 0.7 collective-permute-start.3
  29.7 15.8 %collective-permute-start.4 = (bf16[2,128,128]{2,1,0:T(8,128)(2,1)S(1)}, bf16[2,128,128]{2,1,0:T(8,128)(2,1)S(1)}, u32[]{:S(2)}, u32[]{:S(2)}) collective-permute-start(bf16[2,128,128]{2,1,0:T(8,128)(2,1)S(1)} %broadcast_select_fusion), channel_id=1, source_target_pairs={{0,128},{16,144},{32,160},{48,176},{64,192},{80,208},{96,224},{112... | collective-permute-start | bytes 196616 | tf_op jit(solution)/shard_map/ppermute | solution.py:235
  45.5 1.9 %collective-permute-start.5 = (bf16[2,128,128]{2,1,0:T(8,128)(2,1)S(1)}, bf16[2,128,128]{2,1,0:T(8,128)(2,1)S(1)}, u32[]{:S(2)}, u32[]{:S(2)}) collective-permute-start(bf16[2,128,128]{2,1,0:T(8,128)(2,1)S(1)} %broadcast_select_fusion), channel_id=1, source_target_pairs={{0,256},{16,272},{32,288},{48,304},{64,320},{80,336},{96,352},{112... | collective-permute-start | bytes 196616 | tf_op jit(solution)/shard_map/ppermute | solution.py:235
  47.4 0.0 collective-permute-done.3
  47.5 0.3 collective-permute-done.4
  47.7 7.5 %collective-permute-done.5 = bf16[2,128,128]{2,1,0:T(8,128)(2,1)S(1)} collective-permute-done((bf16[2,128,128]{2,1,0:T(8,128)(2,1)S(1)}, bf16[2,128,128]{2,1,0:T(8,128)(2,1)S(1)}, u32[]{:S(2)}, u32[]{:S(2)}) %collective-permute-start.5) | collective-permute-done | bytes 65568 | tf_op jit(solution)/shard_map/ppermute | solution.py:235
  55.2 0.0 collective-permute-done.6.first_far
  55.2 0.0 collective-permute-done.7.tile_far
  55.2 1.2 %broadcast_in_dim.12 = bf16[16,256,128]{2,1,0:T(8,128)(2,1)} broadcast(bf16[256,128]{1,0:T(8,128)(2,1)S(1)} %pad_maximum_fusion.2), dimensions={1,2} | broadcast | bytes 1114112 | tf_op jit(solution)/shard_map/broadcast_in_dim | solution.py:250
  56.4 0.0 copy-start.1
  56.4 3.8 %all-to-all-start = ((bf16[16,256,128]{2,1,0:T(8,128)(2,1)}), bf16[16,256,128]{2,1,0:T(8,128)(2,1)S(1)}, u32[]{:S(2)}, u32[]{:S(2)}) async-start(bf16[16,256,128]{2,1,0:T(8,128)(2,1)} %broadcast_in_dim.12), calls=%async_computation | async-start | bytes 2097152 | tf_op jit(solution)/shard_map/all_to_all | solution.py:250
  60.2 0.0 copy-done.1
  60.2 4.7 %collective-permute-start.11 = (bf16[2048,128]{1,0:T(8,128)(2,1)S(1)}, bf16[2048,128]{1,0:T(8,128)(2,1)S(1)}, u32[]{:S(2)}, u32[]{:S(2)}) collective-permute-start(bf16[2048,128]{1,0:T(8,128)(2,1)S(1)} %bitcast.30), channel_id=1, source_target_pairs={{0,8},{1,9},{2,10},{3,11},{4,12},{5,13},{6,14},{7,15},{8,0},{9,1},... | collective-permute-start | bytes 1572872 | tf_op jit(solution)/shard_map/ppermute | solution.py:251
  65.0 1.9 %collective-permute-start.8 = (bf16[4,128,128]{2,1,0:T(8,128)(2,1)S(1)}, bf16[4,128,128]{2,1,0:T(8,128)(2,1)S(1)}, u32[]{:S(2)}, u32[]{:S(2)}) collective-permute-start(bf16[4,128,128]{2,1,0:T(8,128)(2,1)S(1)} %get-tuple-element.35), channel_id=1, source_target_pairs={{32,0},{48,16},{64,32},{80,48},{96,64},{112,80},{0,96},{16,112},{1... | collective-permute-start | bytes 393224 | tf_op jit(solution)/shard_map/ppermute | solution.py:261
  66.9 1.9 %collective-permute-start.9 = (bf16[4,128,128]{2,1,0:T(8,128)(2,1)S(1)}, bf16[4,128,128]{2,1,0:T(8,128)(2,1)S(1)}, u32[]{:S(2)}, u32[]{:S(2)}) collective-permute-start(bf16[4,128,128]{2,1,0:T(8,128)(2,1)S(1)} %get-tuple-element.35), channel_id=1, source_target_pairs={{64,0},{80,16},{96,32},{112,48},{0,64},{16,80},{32,96},{48,112},{1... | collective-permute-start | bytes 393224 | tf_op jit(solution)/shard_map/ppermute | solution.py:261
  68.8 5.2 %collective-permute-start.10 = (bf16[4,128,128]{2,1,0:T(8,128)(2,1)S(1)}, bf16[4,128,128]{2,1,0:T(8,128)(2,1)S(1)}, u32[]{:S(2)}, u32[]{:S(2)}) collective-permute-start(bf16[4,128,128]{2,1,0:T(8,128)(2,1)S(1)} %get-tuple-element.35), channel_id=1, source_target_pairs={{96,0},{112,16},{0,32},{16,48},{32,64},{48,80},{64,96},{80,112},{2... | collective-permute-start | bytes 393224 | tf_op jit(solution)/shard_map/ppermute | solution.py:261
  74.0 0.0 collective-permute-done.8
  74.0 5.5 %collective-permute-done.9 = bf16[4,128,128]{2,1,0:T(8,128)(2,1)S(1)} collective-permute-done((bf16[4,128,128]{2,1,0:T(8,128)(2,1)S(1)}, bf16[4,128,128]{2,1,0:T(8,128)(2,1)S(1)}, u32[]{:S(2)}, u32[]{:S(2)}) %collective-permute-start.9) | collective-permute-done | bytes 131104 | tf_op jit(solution)/shard_map/ppermute | solution.py:261
  79.5 0.0 collective-permute-done.10
  79.5 0.1 pad_maximum_fusion.near
  79.6 4.9 %collective-permute-done.11.tile_far = bf16[2048,128]{1,0:T(8,128)(2,1)S(1)} collective-permute-done((bf16[2048,128]{1,0:T(8,128)(2,1)S(1)}, bf16[2048,128]{1,0:T(8,128)(2,1)S(1)}, u32[]{:S(2)}, u32[]{:S(2)}) %collective-permute-start.11) | collective-permute-done | bytes 524320 | tf_op jit(solution)/shard_map/ppermute | solution.py:251
  84.5 2.7 %all-to-all-done.own = bf16[16,256,128]{2,1,0:T(8,128)(2,1)S(1)} async-done(((bf16[16,256,128]{2,1,0:T(8,128)(2,1)}), bf16[16,256,128]{2,1,0:T(8,128)(2,1)S(1)}, u32[]{:S(2)}, u32[]{:S(2)}) %all-to-all-start) | async-done | bytes 1048608 | tf_op jit(solution)/shard_map/all_to_all | solution.py:250
  87.2 3.6 %collective-permute-start.12 = (bf16[4,4,128,128]{3,2,1,0:T(8,128)(2,1)S(1)}, bf16[4,4,128,128]{3,2,1,0:T(8,128)(2,1)S(1)}, u32[]{:S(2)}, u32[]{:S(2)}) collective-permute-start(bf16[4,4,128,128]{3,2,1,0:T(8,128)(2,1)S(1)} %pad_maximum_fusion.near), channel_id=1, source_target_pairs={{0,16},{16,0},{32,48},{48,32},{64,80},{80,64},{96,112},{112,96},{1... | collective-permute-start | bytes 1572872 | tf_op jit(solution)/shard_map/ppermute | solution.py:264
  90.8 2.4 %collective-permute-start.14 = (bf16[4,4,64,128]{3,2,1,0:T(8,128)(2,1)S(1)}, bf16[4,4,64,128]{3,2,1,0:T(8,128)(2,1)S(1)}, u32[]{:S(2)}, u32[]{:S(2)}) collective-permute-start(bf16[4,4,64,128]{3,2,1,0:T(8,128)(2,1)S(1)} %slice.29), channel_id=1, source_target_pairs={{0,8},{1,9},{2,10},{3,11},{4,12},{5,13},{6,14},{7,15},{8,0},{9,1},... | collective-permute-start | bytes 786440 | tf_op jit(solution)/shard_map/ppermute | solution.py:265
  93.3 0.0 collective-permute-done.12.far
  93.3 0.9 shard_map.78.near
  94.2 0.0 copy-start.2
  94.2 4.5 %collective-permute-start.13 = (bf16[128,128]{1,0:T(8,128)(2,1)S(1)}, bf16[128,128]{1,0:T(8,128)(2,1)S(1)}, u32[]{:S(2)}, u32[]{:S(2)}) collective-permute-start(bf16[128,128]{1,0:T(8,128)(2,1)S(1)} %shard_map.78.near), channel_id=1, source_target_pairs={{0,8},{1,9},{2,10},{3,11},{4,12},{5,13},{6,14},{7,15},{8,0},{9,1},... | collective-permute-start | bytes 98312 | tf_op jit(solution)/shard_map/ppermute | solution.py:269
  98.7 3.4 %collective-permute-done.14.near_swapped = bf16[4,4,64,128]{3,2,1,0:T(8,128)(2,1)S(1)} collective-permute-done((bf16[4,4,64,128]{3,2,1,0:T(8,128)(2,1)S(1)}, bf16[4,4,64,128]{3,2,1,0:T(8,128)(2,1)S(1)}, u32[]{:S(2)}, u32[]{:S(2)}) %collective-permute-start.14) | collective-permute-done | bytes 262176 | tf_op jit(solution)/shard_map/ppermute | solution.py:265
  102.1 3.0 %collective-permute-start.15 = (bf16[4,4,64,128]{3,2,1,0:T(8,128)(2,1)S(1)}, bf16[4,4,64,128]{3,2,1,0:T(8,128)(2,1)S(1)}, u32[]{:S(2)}, u32[]{:S(2)}) collective-permute-start(bf16[4,4,64,128]{3,2,1,0:T(8,128)(2,1)S(1)} %collective-permute-done.14.near_swapped), channel_id=1, source_target_pairs={{0,16},{16,0},{32,48},{48,32},{64,80},{80,64},{96,112},{112,96},{1... | collective-permute-start | bytes 786440 | tf_op jit(solution)/shard_map/ppermute | solution.py:266
  105.2 0.0 collective-permute-done.13.far
  105.2 8.2 %shard_map.79 = (bf16[2048,256]{1,0:T(8,128)(2,1)}, f32[256,256]{1,0:T(8,128)S(1)}) custom-call(s32[1,4]{1,0:T(1,128)S(1)} %add_bitcast_fusion.at, bf16[16,256,128]{2,1,0:T(8,128)(2,1)S(1)} %all-to-all-done.own, bf16[128,128]{1,0:T(8,128)(2,1)S(1)} %shard_map.78.near, bf16[128,128]{1,0:T(8,128)(2,1)S(1)} %collective-permute-done.13.far, ...), custom_call_target="tpu_custom_call" | custom-call | flops 8000000000 | bytes 1048576 | tf_op jit(solution)/shard_map/pallas_call | solution.py:187
  113.4 0.0 collective-permute-done.15.far_swapped
  113.4 0.0 copy-done.2
  113.4 2.4 %shard_map.80 = bf16[2048,256]{1,0:T(8,128)(2,1)} custom-call(s32[1,4]{1,0:T(1,128)S(1)} %add_bitcast_fusion.at, bf16[2048,128]{1,0:T(8,128)(2,1)S(1)} %bitcast.33, bf16[2048,128]{1,0:T(8,128)(2,1)S(1)} %collective-permute-done.7.tile_far, f32[264,128]{1,0:T(8,128)S(1)} %shard_map.77.first_near, f32[264,128]{1,0:T(8,128)S(1)} %collective-permute-done.6.first_far, ...), custom_call_target="tpu_custom_call" | custom-call | flops 2000000000 | bytes 1048576 | tf_op jit(solution)/shard_map/pallas_call | solution.py:187
  (7 shorter events, 0.1 us)
Async XLA Ops:
  1.5 23.5 %collective-permute-start.1 = (bf16[128,128]{1,0:T(8,128)(2,1)S(1)}, bf16[128,128]{1,0:T(8,128)(2,1)S(1)}, u32[]{:S(2)}, u32[]{:S(2)}) collective-permute-start(bf16[128,128]{1,0:T(8,128)(2,1)S(1)} %get-tuple-element.41), channel_id=1, source_target_pairs={{0,16},{1,0},{2,48},{3,32},{4,80},{5,64},{6,112},{7,96},{8,144},{9... | collective-permute-start | bytes 98312 | tf_op jit(solution)/shard_map/ppermute | solution.py:210
  4.9 20.0 %collective-permute-start = (bf16[128,128]{1,0:T(8,128)(2,1)S(1)}, bf16[128,128]{1,0:T(8,128)(2,1)S(1)}, u32[]{:S(2)}, u32[]{:S(2)}) collective-permute-start(bf16[128,128]{1,0:T(8,128)(2,1)S(1)} %get-tuple-element.40), channel_id=1, source_target_pairs={{0,0},{1,16},{2,32},{3,48},{4,64},{5,80},{6,96},{7,112},{8,128},{9... | collective-permute-start | bytes 98312 | tf_op jit(solution)/shard_map/ppermute | solution.py:210
  13.0 42.2 %collective-permute-start.7 = (bf16[2048,128]{1,0:T(8,128)(2,1)}, bf16[2048,128]{1,0:T(8,128)(2,1)S(1)}, u32[]{:S(2)}, u32[]{:S(2)}) collective-permute-start(bf16[2048,128]{1,0:T(8,128)(2,1)} %bitcast.32), channel_id=1, source_target_pairs={{0,8},{1,9},{2,10},{3,11},{4,12},{5,13},{6,14},{7,15},{8,0},{9,1},... | collective-permute-start | bytes 1572872 | tf_op jit(solution)/shard_map/ppermute | solution.py:237
  18.5 1.0 copy-start
  25.0 4.0 %collective-permute-start.2 = (bf16[2,128,128]{2,1,0:T(8,128)(2,1)S(1)}, bf16[2,128,128]{2,1,0:T(8,128)(2,1)S(1)}, u32[]{:S(2)}, u32[]{:S(2)}) collective-permute-start(bf16[2,128,128]{2,1,0:T(8,128)(2,1)S(1)} %maximum_select_fusion), channel_id=1, source_target_pairs={{0,384},{16,400},{32,416},{48,432},{64,448},{80,464},{96,480},{112... | collective-permute-start | bytes 196616 | tf_op jit(solution)/shard_map/ppermute | solution.py:225
  26.3 28.9 %collective-permute-start.6 = (f32[264,128]{1,0:T(8,128)S(1)}, f32[264,128]{1,0:T(8,128)S(1)}, u32[]{:S(2)}, u32[]{:S(2)}) collective-permute-start(f32[264,128]{1,0:T(8,128)S(1)} %shard_map.77.first_near), channel_id=1, source_target_pairs={{0,8},{1,9},{2,10},{3,11},{4,12},{5,13},{6,14},{7,15},{8,0},{9,1},... | collective-permute-start | bytes 405512 | tf_op jit(solution)/shard_map/ppermute | solution.py:236
  29.1 18.4 %collective-permute-start.3 = (bf16[2,128,128]{2,1,0:T(8,128)(2,1)S(1)}, bf16[2,128,128]{2,1,0:T(8,128)(2,1)S(1)}, u32[]{:S(2)}, u32[]{:S(2)}) collective-permute-start(bf16[2,128,128]{2,1,0:T(8,128)(2,1)S(1)} %broadcast_select_fusion), channel_id=1, source_target_pairs={{0,0},{16,16},{32,32},{48,48},{64,64},{80,80},{96,96},{112,112},{1... | collective-permute-start | bytes 196616 | tf_op jit(solution)/shard_map/ppermute | solution.py:235
  29.7 18.0 %collective-permute-start.4 = (bf16[2,128,128]{2,1,0:T(8,128)(2,1)S(1)}, bf16[2,128,128]{2,1,0:T(8,128)(2,1)S(1)}, u32[]{:S(2)}, u32[]{:S(2)}) collective-permute-start(bf16[2,128,128]{2,1,0:T(8,128)(2,1)S(1)} %broadcast_select_fusion), channel_id=1, source_target_pairs={{0,128},{16,144},{32,160},{48,176},{64,192},{80,208},{96,224},{112... | collective-permute-start | bytes 196616 | tf_op jit(solution)/shard_map/ppermute | solution.py:235
  45.5 9.7 %collective-permute-start.5 = (bf16[2,128,128]{2,1,0:T(8,128)(2,1)S(1)}, bf16[2,128,128]{2,1,0:T(8,128)(2,1)S(1)}, u32[]{:S(2)}, u32[]{:S(2)}) collective-permute-start(bf16[2,128,128]{2,1,0:T(8,128)(2,1)S(1)} %broadcast_select_fusion), channel_id=1, source_target_pairs={{0,256},{16,272},{32,288},{48,304},{64,320},{80,336},{96,352},{112... | collective-permute-start | bytes 196616 | tf_op jit(solution)/shard_map/ppermute | solution.py:235
  56.4 3.8 %copy-start.1 = (bf16[1,1,2048,128]{3,2,1,0:T(8,128)(2,1)S(1)}, bf16[1,1,2048,128]{3,2,1,0:T(8,128)(2,1)}, u32[]{:S(2)}) copy-start(bf16[1,1,2048,128]{3,2,1,0:T(8,128)(2,1)} %param.6) | copy-start | bytes 1572868
  56.4 30.8 %all-to-all-start = ((bf16[16,256,128]{2,1,0:T(8,128)(2,1)}), bf16[16,256,128]{2,1,0:T(8,128)(2,1)S(1)}, u32[]{:S(2)}, u32[]{:S(2)}) async-start(bf16[16,256,128]{2,1,0:T(8,128)(2,1)} %broadcast_in_dim.12), calls=%async_computation | async-start | bytes 2097152 | tf_op jit(solution)/shard_map/all_to_all | solution.py:250
  60.2 24.2 %collective-permute-start.11 = (bf16[2048,128]{1,0:T(8,128)(2,1)S(1)}, bf16[2048,128]{1,0:T(8,128)(2,1)S(1)}, u32[]{:S(2)}, u32[]{:S(2)}) collective-permute-start(bf16[2048,128]{1,0:T(8,128)(2,1)S(1)} %bitcast.30), channel_id=1, source_target_pairs={{0,8},{1,9},{2,10},{3,11},{4,12},{5,13},{6,14},{7,15},{8,0},{9,1},... | collective-permute-start | bytes 1572872 | tf_op jit(solution)/shard_map/ppermute | solution.py:251
  65.0 9.0 %collective-permute-start.8 = (bf16[4,128,128]{2,1,0:T(8,128)(2,1)S(1)}, bf16[4,128,128]{2,1,0:T(8,128)(2,1)S(1)}, u32[]{:S(2)}, u32[]{:S(2)}) collective-permute-start(bf16[4,128,128]{2,1,0:T(8,128)(2,1)S(1)} %get-tuple-element.35), channel_id=1, source_target_pairs={{32,0},{48,16},{64,32},{80,48},{96,64},{112,80},{0,96},{16,112},{1... | collective-permute-start | bytes 393224 | tf_op jit(solution)/shard_map/ppermute | solution.py:261
  66.9 12.6 %collective-permute-start.9 = (bf16[4,128,128]{2,1,0:T(8,128)(2,1)S(1)}, bf16[4,128,128]{2,1,0:T(8,128)(2,1)S(1)}, u32[]{:S(2)}, u32[]{:S(2)}) collective-permute-start(bf16[4,128,128]{2,1,0:T(8,128)(2,1)S(1)} %get-tuple-element.35), channel_id=1, source_target_pairs={{64,0},{80,16},{96,32},{112,48},{0,64},{16,80},{32,96},{48,112},{1... | collective-permute-start | bytes 393224 | tf_op jit(solution)/shard_map/ppermute | solution.py:261
  68.8 10.7 %collective-permute-start.10 = (bf16[4,128,128]{2,1,0:T(8,128)(2,1)S(1)}, bf16[4,128,128]{2,1,0:T(8,128)(2,1)S(1)}, u32[]{:S(2)}, u32[]{:S(2)}) collective-permute-start(bf16[4,128,128]{2,1,0:T(8,128)(2,1)S(1)} %get-tuple-element.35), channel_id=1, source_target_pairs={{96,0},{112,16},{0,32},{16,48},{32,64},{48,80},{64,96},{80,112},{2... | collective-permute-start | bytes 393224 | tf_op jit(solution)/shard_map/ppermute | solution.py:261
  87.2 6.1 %collective-permute-start.12 = (bf16[4,4,128,128]{3,2,1,0:T(8,128)(2,1)S(1)}, bf16[4,4,128,128]{3,2,1,0:T(8,128)(2,1)S(1)}, u32[]{:S(2)}, u32[]{:S(2)}) collective-permute-start(bf16[4,4,128,128]{3,2,1,0:T(8,128)(2,1)S(1)} %pad_maximum_fusion.near), channel_id=1, source_target_pairs={{0,16},{16,0},{32,48},{48,32},{64,80},{80,64},{96,112},{112,96},{1... | collective-permute-start | bytes 1572872 | tf_op jit(solution)/shard_map/ppermute | solution.py:264
  90.8 11.3 %collective-permute-start.14 = (bf16[4,4,64,128]{3,2,1,0:T(8,128)(2,1)S(1)}, bf16[4,4,64,128]{3,2,1,0:T(8,128)(2,1)S(1)}, u32[]{:S(2)}, u32[]{:S(2)}) collective-permute-start(bf16[4,4,64,128]{3,2,1,0:T(8,128)(2,1)S(1)} %slice.29), channel_id=1, source_target_pairs={{0,8},{1,9},{2,10},{3,11},{4,12},{5,13},{6,14},{7,15},{8,0},{9,1},... | collective-permute-start | bytes 786440 | tf_op jit(solution)/shard_map/ppermute | solution.py:265
  94.2 19.2 %copy-start.2 = (bf16[1,1,2048,128]{3,2,1,0:T(8,128)(2,1)S(1)}, bf16[1,1,2048,128]{3,2,1,0:T(8,128)(2,1)}, u32[]{:S(2)}) copy-start(bf16[1,1,2048,128]{3,2,1,0:T(8,128)(2,1)} %param.7) | copy-start | bytes 1572868
  94.2 11.0 %collective-permute-start.13 = (bf16[128,128]{1,0:T(8,128)(2,1)S(1)}, bf16[128,128]{1,0:T(8,128)(2,1)S(1)}, u32[]{:S(2)}, u32[]{:S(2)}) collective-permute-start(bf16[128,128]{1,0:T(8,128)(2,1)S(1)} %shard_map.78.near), channel_id=1, source_target_pairs={{0,8},{1,9},{2,10},{3,11},{4,12},{5,13},{6,14},{7,15},{8,0},{9,1},... | collective-permute-start | bytes 98312 | tf_op jit(solution)/shard_map/ppermute | solution.py:269
  102.1 11.2 %collective-permute-start.15 = (bf16[4,4,64,128]{3,2,1,0:T(8,128)(2,1)S(1)}, bf16[4,4,64,128]{3,2,1,0:T(8,128)(2,1)S(1)}, u32[]{:S(2)}, u32[]{:S(2)}) collective-permute-start(bf16[4,4,64,128]{3,2,1,0:T(8,128)(2,1)S(1)} %collective-permute-done.14.near_swapped), channel_id=1, source_target_pairs={{0,16},{16,0},{32,48},{48,32},{64,80},{80,64},{96,112},{112,96},{1... | collective-permute-start | bytes 786440 | tf_op jit(solution)/shard_map/ppermute | solution.py:266
